TPU v7x, 256 devices: a whole 4x4x8 slice. The times are simulated.
256 devices in a mesh: section: 2 (over z_hi), dp: 8 (over z_lo, core), mp: 16 (over x, y).
Axes of the slice: x: 4, y: 4, z: 8 (z_hi: 2, z_lo: 4; z = z_hi * 4 + z_lo), core: 2. Of those that a mesh axis runs over, the one named last changes fastest.
Arguments:
- queries: bfloat16 [64, 4, 8192], P('dp'), may hold values from -48 to 48
- new_keys: bfloat16 [64, 4, 1024], P('dp'), may hold values from -6 to 6
- new_values: bfloat16 [64, 4, 1024], P('dp'), may hold values from -6 to 6
- cache_keys: bfloat16 [64, 512, 1024], P('dp', 'mp'), may hold values from -32 to 32
- cache_values: bfloat16 [64, 512, 1024], P('dp', 'mp'), may hold values from -6 to 6
- lengths: int32 [64], P('dp'), may hold values from 2 to 512, as said below
- out_weight: bfloat16 [8192, 8192], P('mp', ('section', 'dp')), may hold values from -0.0625 to 0.0625
- resid_expert: bfloat16 [256, 8192], P(None, ('section', 'dp')), may hold values from -8 to 8
- gain_expert: bfloat16 [8192], P(('section', 'dp')), may hold values from 0.25 to 1.75
- hidden_amateur: bfloat16 [256, 4096], P(None, ('section', 'dp')), may hold values from -8 to 8
- gain_amateur: bfloat16 [4096], P(('section', 'dp')), may hold values from 0.25 to 1.75
- head_expert: bfloat16 [131072, 8192], P(('section', 'dp', 'mp')), may hold values from -0.34250485 to 0.34250485
- head_amateur: bfloat16 [131072, 4096], P(('section', 'dp', 'mp')), may hold values from -0.484375 to 0.484375
- chosen: int32 [64, 4], replicated, may hold values from 0 to 131071
Outputs:
- scores: bfloat16 [64, 4, 131072], P(None, None, ('section', 'dp', 'mp'))
- chosen_score: float32 [64, 4], replicated
Inputs may be any that keep to these rules, and one draw needn't show every extreme that they name: `lengths`: some sequence has 512 cached positions.
All inputs are finite; a program needn't handle non-finite values.
Results may differ from a plain program's by a relative error of at most 0.0034.
Values may be sent and summed in bfloat16 or wider, within the bound.
A program may use at most 128 MiB of HBM per device.

v0:
```python
import jax
import jax.numpy as jnp
from jax import lax
from jax.sharding import PartitionSpec as P

KVH = 8
HD = 128


CONTRAST = 0.5
NEGATIVE = -1e30
EPSILON = 1e-05


def merged(array, axis, combine):
    everything = jax.tree.map(lambda part: lax.all_gather(part, axis), array)
    initial = jax.tree.map(lambda part: part[0], everything)

    def hop(k, so_far):
        return combine(so_far, jax.tree.map(lambda part: part[k], everything))

    return lax.fori_loop(1, lax.axis_size(axis), hop, initial)


def normalize(hidden, gain_vector):
    widened = hidden.astype(jnp.float32)
    mean_sq = jnp.mean(widened * widened, axis=1, keepdims=True)
    return (widened * lax.rsqrt(mean_sq + EPSILON) * gain_vector.astype(jnp.float32)).astype(
        jnp.bfloat16
    )


def partial_attention(
    queries, new_keys, new_values, cache_keys, cache_values, lengths, offset, with_new
):
    row_count = queries.shape[0]
    step_count = queries.shape[1]
    span_len = cache_keys.shape[1]
    group_size = queries.shape[2] // (KVH * HD)
    query_all = queries.reshape(row_count, step_count, KVH, group_size, HD)
    keys_old = cache_keys.reshape(row_count, span_len, KVH, HD)
    values_old = cache_values.astype(jnp.float32).reshape(row_count, span_len, KVH, HD)
    keys_new = new_keys.reshape(row_count, step_count, KVH, HD)
    values_new = new_values.astype(jnp.float32).reshape(row_count, step_count, KVH, HD)
    scaling = 1.0 / HD**0.5
    scores_old = (
        jnp.einsum("rsghd,rpgd->rsghp", query_all, keys_old, preferred_element_type=jnp.float32)
        * scaling
    )
    scores_new = (
        jnp.einsum("rsghd,rtgd->rsght", query_all, keys_new, preferred_element_type=jnp.float32)
        * scaling
    )
    positions = offset + jnp.arange(span_len, dtype=jnp.int32)
    live_old = (positions[None, :] < lengths[:, None])[:, None, None, None, :]
    step_order = jnp.arange(step_count, dtype=jnp.int32)
    live_new = ((step_order[None, :] <= step_order[:, None]) & with_new)[None, :, None, None, :]
    scores_old = jnp.where(live_old, scores_old, NEGATIVE)
    scores_new = jnp.where(live_new, scores_new, NEGATIVE)
    column_max = jnp.maximum(jnp.max(scores_old, axis=-1), jnp.max(scores_new, axis=-1))
    weights_old = jnp.where(live_old, jnp.exp(scores_old - column_max[..., None]), 0.0)
    weights_new = jnp.where(live_new, jnp.exp(scores_new - column_max[..., None]), 0.0)
    totals = jnp.sum(weights_old, axis=-1) + jnp.sum(weights_new, axis=-1)
    mixture = jnp.einsum(
        "rsghp,rpgd->rsghd", weights_old, values_old, precision=lax.Precision.HIGHEST
    )
    mixture = mixture + jnp.einsum(
        "rsght,rtgd->rsghd", weights_new, values_new, precision=lax.Precision.HIGHEST
    )
    head_count = KVH * group_size
    return (
        column_max.reshape(row_count, step_count, head_count),
        totals.reshape(row_count, step_count, head_count),
        mixture.reshape(row_count, step_count, head_count, HD),
    )


def join_heads(first_part, second_part):
    top_value = jnp.maximum(first_part[0], second_part[0])
    first_scale = jnp.exp(first_part[0] - top_value)
    second_scale = jnp.exp(second_part[0] - top_value)
    return (
        top_value,
        first_part[1] * first_scale + second_part[1] * second_scale,
        first_part[2] * first_scale[..., None] + second_part[2] * second_scale[..., None],
    )


def join_vocab(first_part, second_part):
    top_expert = jnp.maximum(first_part[0], second_part[0])
    top_amateur = jnp.maximum(first_part[2], second_part[2])
    total_expert = first_part[1] * jnp.exp(first_part[0] - top_expert) + second_part[1] * jnp.exp(
        second_part[0] - top_expert
    )
    total_amateur = first_part[3] * jnp.exp(first_part[2] - top_amateur) + second_part[3] * jnp.exp(
        second_part[2] - top_amateur
    )
    return (top_expert, total_expert, top_amateur, total_amateur, first_part[4] + second_part[4])


def local(
    queries,
    new_keys,
    new_values,
    cache_keys,
    cache_values,
    lengths,
    out_weight,
    resid_expert,
    gain_expert,
    hidden_amateur,
    gain_amateur,
    head_expert,
    head_amateur,
    chosen,
):
    mp_index = lax.axis_index("mp")
    span_len = cache_keys.shape[1]
    column_max, totals, mixture = partial_attention(
        queries,
        new_keys,
        new_values,
        cache_keys,
        cache_values,
        lengths,
        mp_index * span_len,
        mp_index == 0,
    )
    local_heads = queries.shape[2] // HD // lax.axis_size("mp")
    column_max, totals, mixture = merged((column_max, totals, mixture), "mp", join_heads)
    totals = lax.dynamic_slice_in_dim(totals, mp_index * local_heads, local_heads, 2)
    mixture = lax.dynamic_slice_in_dim(mixture, mp_index * local_heads, local_heads, 2)
    attended = (mixture / totals[..., None]).astype(jnp.bfloat16)
    attended = attended.reshape(-1, local_heads * HD)
    partial_sum = jnp.dot(
        lax.all_gather(attended, "dp", axis=0, tiled=True),
        out_weight,
        preferred_element_type=jnp.float32,
    )
    projected = lax.psum(partial_sum, "mp")
    hidden_expert = (resid_expert.astype(jnp.float32) + projected).astype(jnp.bfloat16)
    full_expert, full_gain_expert, full_amateur, full_gain_amateur = (
        lax.all_gather(hidden_expert, ("section", "dp"), axis=1, tiled=True),
        lax.all_gather(gain_expert, ("section", "dp"), axis=0, tiled=True),
        lax.all_gather(hidden_amateur, ("section", "dp"), axis=1, tiled=True),
        lax.all_gather(gain_amateur, ("section", "dp"), axis=0, tiled=True),
    )
    normed_expert = normalize(full_expert, full_gain_expert)
    normed_amateur = normalize(full_amateur, full_gain_amateur)
    vocab_width = head_expert.shape[0]
    vocab_start = lax.axis_index(("section", "dp", "mp")) * vocab_width
    logits_expert = lax.dot_general(
        normed_expert, head_expert, (((1,), (1,)), ((), ())), preferred_element_type=jnp.float32
    )
    logits_amateur = lax.dot_general(
        normed_amateur, head_amateur, (((1,), (1,)), ((), ())), preferred_element_type=jnp.float32
    )
    target = chosen.reshape(-1) - vocab_start
    matched = target[:, None] == jnp.arange(vocab_width, dtype=jnp.int32)[None, :]
    difference = logits_expert - CONTRAST * logits_amateur
    picked = jnp.sum(jnp.where(matched, difference, 0.0), axis=1)
    peak_expert = jnp.max(logits_expert, axis=1)
    total_expert = jnp.sum(jnp.exp(logits_expert - peak_expert[:, None]), axis=1)
    peak_amateur = jnp.max(logits_amateur, axis=1)
    total_amateur = jnp.sum(jnp.exp(logits_amateur - peak_amateur[:, None]), axis=1)
    peak_expert, total_expert, peak_amateur, total_amateur, picked = merged(
        (peak_expert, total_expert, peak_amateur, total_amateur, picked),
        ("section", "dp", "mp"),
        join_vocab,
    )
    lse_expert = peak_expert + jnp.log(total_expert)
    lse_amateur = peak_amateur + jnp.log(total_amateur)
    contrast_all = (
        logits_expert - lse_expert[:, None] - CONTRAST * (logits_amateur - lse_amateur[:, None])
    )
    scores = contrast_all.astype(jnp.bfloat16).reshape(
        chosen.shape[0], chosen.shape[1], vocab_width
    )
    chosen_score = (picked - lse_expert + CONTRAST * lse_amateur).reshape(
        chosen.shape[0], chosen.shape[1]
    )
    return (scores, chosen_score)


def solution(mesh):
    return jax.shard_map(
        local,
        mesh=mesh,
        in_specs=(
            P("dp", None, None),
            P("dp", None, None),
            P("dp", None, None),
            P("dp", "mp", None),
            P("dp", "mp", None),
            P("dp"),
            P("mp", ("section", "dp")),
            P(None, ("section", "dp")),
            P(("section", "dp")),
            P(None, ("section", "dp")),
            P(("section", "dp")),
            P(("section", "dp", "mp"), None),
            P(("section", "dp", "mp"), None),
            P(),
        ),
        out_specs=(P(None, None, ("section", "dp", "mp")), P()),
        check_vma=False,
    )
```

profile of v0, /device:TPU:1, one launch (start us, length us, event | category | flops | bytes accessed | tf_op | source)
XLA Modules:
  0.0 886.2 jit_solution(5572272225074035743)
XLA Ops:
  12.8 2.5 fusion.44
  19.9 20.2 %all_gather.55 = f32[16,8,4,64]{3,1,2,0:T(8,128)S(1)} all-gather(f32[1,8,4,64]{3,1,2,0:T(8,128)S(1)} %add.194), channel_id=1, replica_groups=mesh['section'=2,'dp'=8,'mp'=16] {'mp'}, dimensions={0}, use_global_device_ids=true | all-gather | bytes 139264 | tf_op jit(solution)/shard_map/all_gather | solution.py:16
  40.2 19.7 %all_gather.54 = f32[16,8,4,64]{3,1,2,0:T(8,128)S(1)} all-gather(f32[1,8,4,64]{3,1,2,0:T(8,128)S(1)} %max.48), channel_id=1, replica_groups=mesh['section'=2,'dp'=8,'mp'=16] {'mp'}, dimensions={0}, use_global_device_ids=true | all-gather | bytes 139264 | tf_op jit(solution)/shard_map/all_gather | solution.py:16
  59.9 79.8 %all-gather.16.cloned.1.call-done = f32[16,8,4,64,128]{4,3,2,1,0:T(8,128)} async-done(((f32[1,8,4,64,128]{4,3,2,1,0:T(8,128)}), f32[16,8,4,64,128]{4,3,2,1,0:T(8,128)}) %all-gather.16.cloned.1.call-update) | async-done | bytes 16777232 | tf_op jit(solution)/shard_map/all_gather | solution.py:16
  141.1 34.0 %while.42 = (s32[]{:T(128)}, f32[8,4,64]{2,1,0:T(4,128)S(1)}, f32[8,4,64]{2,1,0:T(4,128)S(1)}, f32[8,4,64,128]{3,2,1,0:T(8,128)S(1)}, f32[16,8,4,64]{3,1,2,0:T(8...) while((s32[]{:T(128)}, f32[8,4,64]{2,1,0:T(4,128)S(1)}, ...), condition=%wide.region_5.6_spmd, body=%wide.region_4.5_spmd.sunk | while | flops 798725 | bytes 3260567 | solution.py:22
  141.2 2.2 fusion.55
  143.5 2.2 fusion.55
  145.7 2.2 fusion.55
  148.0 2.2 fusion.55
  150.3 2.2 fusion.55
  163.8 2.2 fusion.55
  175.3 15.0 %all_gather.57 = bf16[256,512]{1,0:T(8,128)(2,1)S(1)} all-gather(bf16[32,512]{1,0:T(8,128)(2,1)S(1)} %bitcast.142), channel_id=1, replica_groups=mesh['section'=2,'dp'=8,'mp'=16] {'dp'}, dimensions={0}, use_global_device_ids=true | all-gather | bytes 294912 | tf_op jit(solution)/shard_map/all_gather | solution.py:136
  192.0 92.6 %all-reduce.2.cloned.1.call-done = f32[256,512]{1,0:T(8,128)} async-done(((f32[256,512]{1,0:T(8,128)}), f32[256,512]{1,0:T(8,128)}) %all-reduce.2.cloned.1.call-update) | async-done | bytes 524304 | tf_op jit(solution)/shard_map/psum | solution.py:140
  286.5 19.4 %all-gather.5 = bf16[16,1,512]{2,1,0:T(2,128)(2,1)S(1)} all-gather(bf16[1,1,512]{2,1,0:T(2,128)(2,1)S(1)} %reshape.165), channel_id=1, replica_groups=mesh['section'=2,'dp'=8,'mp'=16] {'section','dp'}, dimensions={0}, use_global_device_ids=true | all-gather | bytes 17408 | tf_op jit(solution)/shard_map/all_gather | solution.py:144
  306.2 15.1 %all-gather.8 = bf16[16,1,256]{2,1,0:T(2,128)(2,1)S(1)} all-gather(bf16[1,1,256]{2,1,0:T(2,128)(2,1)S(1)} %reshape.171), channel_id=1, replica_groups=mesh['section'=2,'dp'=8,'mp'=16] {'section','dp'}, dimensions={0}, use_global_device_ids=true | all-gather | bytes 8704 | tf_op jit(solution)/shard_map/all_gather | solution.py:146
  323.5 4.2 fusion.46
  327.7 100.2 %all-gather.9 = f32[256,1,256]{2,1,0:T(1,128)S(1)} all-gather(f32[1,1,256]{2,1,0:T(1,128)S(1)} %bitcast.155), channel_id=4, replica_groups=mesh['section'=2,'dp'=8,'mp'=16] {'section','dp','mp'}, dimensions={0}, use_global_device_ids=true | all-gather | bytes 263168 | tf_op jit(solution)/shard_map/all_gather | solution.py:16
  428.0 3.3 fusion.4
  431.5 5.8 fusion.45
  437.8 101.2 %all-gather.7 = f32[256,1,256]{2,1,0:T(1,128)S(1)} all-gather(f32[1,1,256]{2,1,0:T(1,128)S(1)} %bitcast.158), channel_id=3, replica_groups=mesh['section'=2,'dp'=8,'mp'=16] {'section','dp','mp'}, dimensions={0}, use_global_device_ids=true | all-gather | bytes 263168 | tf_op jit(solution)/shard_map/all_gather | solution.py:16
  539.0 101.3 %all-gather.10 = f32[256,1,256]{2,1,0:T(1,128)S(1)} all-gather(f32[1,1,256]{2,1,0:T(1,128)S(1)} %bitcast.157), channel_id=5, replica_groups=mesh['section'=2,'dp'=8,'mp'=16] {'section','dp','mp'}, dimensions={0}, use_global_device_ids=true | all-gather | bytes 263168 | tf_op jit(solution)/shard_map/all_gather | solution.py:16
  640.3 101.3 %all-gather.11 = f32[256,1,256]{2,1,0:T(1,128)S(1)} all-gather(f32[1,1,256]{2,1,0:T(1,128)S(1)} %bitcast.156), channel_id=6, replica_groups=mesh['section'=2,'dp'=8,'mp'=16] {'section','dp','mp'}, dimensions={0}, use_global_device_ids=true | all-gather | bytes 263168 | tf_op jit(solution)/shard_map/all_gather | solution.py:16
  741.6 101.3 %all-gather.6 = f32[256,1,256]{2,1,0:T(1,128)S(1)} all-gather(f32[1,1,256]{2,1,0:T(1,128)S(1)} %bitcast.154), channel_id=2, replica_groups=mesh['section'=2,'dp'=8,'mp'=16] {'section','dp','mp'}, dimensions={0}, use_global_device_ids=true | all-gather | bytes 263168 | tf_op jit(solution)/shard_map/all_gather | solution.py:16
  843.0 34.1 %while.43 = (s32[]{:T(128)}, f32[256]{0:T(256)S(1)}, f32[256]{0:T(256)S(1)}, f32[256]{0:T(256)S(1)}, f32[256]{0:T(256)S(1)}, /*index=5*/f32[256]{0:T(256)S(1)}, ...) while((s32[]{:T(128)}, f32[256]{0:T(256)S(1)}, ...), condition=%wide.region_15.16_spmd, body=%wide.region_14.15_spmd.sunk | while | flops 3333 | bytes 25787 | solution.py:22
  (1656 shorter events, 61.9 us)
Async XLA Ops:
  8.0 182.3 %copy-start = (bf16[512,512]{1,0:T(8,128)(2,1)S(1)}, bf16[512,512]{1,0:T(8,128)(2,1)}, u32[]{:S(2)}) copy-start(bf16[512,512]{1,0:T(8,128)(2,1)} %param.24) | copy-start | bytes 1572868
  8.0 4.2 copy-start.7
  8.0 4.8 copy-start.8
  8.0 131.7 %all-gather.16.cloned.1.call-start = ((), (), s32[]{:S(2)}) async-start(), calls=%async_computation | async-start | bytes 17825792 | tf_op jit(solution)/shard_map/all_gather | solution.py:16
  9.7 5.6 copy-start.4
  18.4 266.2 %all-reduce.2.cloned.1.call-start = ((), (), s32[]{:S(2)}) async-start(), calls=%async_computation.1 | async-start | bytes 1048576 | tf_op jit(solution)/shard_map/psum | solution.py:140
  141.1 143.6 %copy-start.3 = (bf16[256,512]{1,0:T(8,128)(2,1)S(1)}, bf16[256,512]{1,0:T(8,128)(2,1)}, u32[]{:S(2)}) copy-start(bf16[256,512]{1,0:T(8,128)(2,1)} %param.25) | copy-start | bytes 786436
  141.1 145.4 %copy-start.6 = (bf16[512]{0:T(512)(128)(2,1)S(1)}, bf16[512]{0:T(512)(128)(2,1)}, u32[]{:S(2)}) copy-start(bf16[512]{0:T(512)(128)(2,1)} %param.26) | copy-start | bytes 3076
  141.1 164.8 %copy-start.5 = (s32[64,4]{0,1:T(4,128)S(1)}, s32[64,4]{0,1:T(4,128)}, u32[]{:S(2)}) copy-start(s32[64,4]{0,1:T(4,128)} %param.31) | copy-start | bytes 3076
  141.1 165.1 %copy-start.9 = (bf16[256]{0:T(256)(128)(2,1)S(1)}, bf16[256]{0:T(256)(128)(2,1)}, u32[]{:S(2)}) copy-start(bf16[256]{0:T(256)(128)(2,1)} %param.28) | copy-start | bytes 1540
  191.4 130.0 %all-gather.20.cloned.1.call-start = ((), (), s32[]{:S(2)}) async-start(), calls=%async_computation.3 | async-start | bytes 2228224 | tf_op jit(solution)/shard_map/all_gather | solution.py:145
  192.0 236.0 %all-gather.18.cloned.1.call-start = ((), (), s32[]{:S(2)}) async-start(), calls=%async_computation.2 | async-start | bytes 4456448 | tf_op jit(solution)/shard_map/all_gather | solution.py:143
  427.9 9.4 %copy-start.2 = (f32[256,1,256]{2,1,0:T(1,128)}, f32[256,1,256]{2,1,0:T(1,128)S(1)}, u32[]{:S(2)}) copy-start(f32[256,1,256]{2,1,0:T(1,128)S(1)} %all-gather.9) | copy-start | bytes 786436
  428.0 3.5 copy-start.1
  437.3 405.6 %slice-start = ((f32[256,1,256]{2,1,0:T(1,128)}), f32[1,1,256]{2,1,0:T(1,128)S(1)}, s32[]{:S(2)}) async-start(f32[256,1,256]{2,1,0:T(1,128)} %copy-done.2), calls=%async_computation.4 | async-start | bytes 2048 | tf_op jit(solution)/shard_map/slice | solution.py:17
Sparse Core Ops, SparseCore 0:
  18.5 121.1 all-gather.15
  191.5 93.0 all-reduce.1
Sparse Core Ops, SparseCore 1:
  193.6 40.3 all-gather.19
  286.6 43.4 all-gather.17
where the time goes:
time: 887 us; the launch traced here: 886 us
  blocking collectives  595 us (67%)
  waiting for transfers between devices  173 us (20%)
  other arithmetic  55.5 us (6%)
  local copies, waits for them, and re-layouts  18.4 us (2%)
  matrix products  16.1 us (2%)
  between operations  16 us (2%)
  loops' own time  12.4 us (1%)
    all_gather x7, blocking collectives, merged(): everything = jax.tree.map(lambda part: lax.all_gather(part, axis), array)  545 us
    psum x1, waiting for transfers between devices, local(): projected = lax.psum(partial_sum, 'mp')  92.6 us
    all_gather x1, waiting for transfers between devices, merged(): everything = jax.tree.map(lambda part: lax.all_gather(part, axis), array)  79.8 us
    add x15, other arithmetic, join_heads(): first_part[2] * first_scale[..., None]  32.8 us
    all_gather x1, blocking collectives, local(): lax.all_gather(gain_expert, ('section', 'dp'), axis=0, tiled=True)  19.4 us
  transfers between devices with their start and end apart: 4, of which 2 were waited for; matrix products, arithmetic and copies ran while one was open for 1% of the time, Pallas kernels for 0%

commit v1 on v0

v1 whole, which is shorter than its diff:
```python
import jax
import jax.numpy as jnp
from jax import lax
from jax.experimental import pallas as pl
from jax.experimental.pallas import tpu as pltpu
from jax.sharding import PartitionSpec as P

MESH = pl.DeviceIdType.MESH
F32 = jnp.float32
BF16 = jnp.bfloat16
KVH = 8
HD = 128
CONTRAST = 0.5
NEGATIVE = -1e30
EPSILON = 1e-05
NT = (((1,), (1,)), ((), ()))
TN = (((0,), (0,)), ((), ()))


def rcopy(src, dst, send_sem, recv_sem, device):
    return pltpu.make_async_remote_copy(
        src_ref=src,
        dst_ref=dst,
        send_sem=send_sem,
        recv_sem=recv_sem,
        device_id=device,
        device_id_type=MESH,
    )


def iota(shape, dim):
    return lax.broadcasted_iota(jnp.int32, shape, dim)


def kernel(
    lengths,
    queries,
    new_keys,
    new_values,
    resid,
    gain_expert,
    gain_amateur,
    hidden_amateur,
    chosen,
    cache_keys,
    cache_values,
    out_weight,
    head_expert,
    head_amateur,
    out,
    out_chosen,
    keys_v,
    values_v,
    weight_v,
    he_v,
    ha_v,
    state_out,
    state_in,
    scale_t,
    attended,
    part_out,
    part_in,
    full,
    amateur,
    acc_e,
    acc_a,
    square_e,
    square_a,
    diff,
    stats_p,
    stats_z,
    load_sem,
    state_sem,
    attended_sem,
    part_sem,
    one_sem,
    two_sem,
    three_send,
    three_recv,
    relay_send,
    relay_recv,
    am_send,
    am_recv,
    am_rsend,
    am_rrecv,
    stats_sem,
):
    sec = lax.axis_index("section")
    dp = lax.axis_index("dp")
    mp = lax.axis_index("mp")
    z = sec * 4 + dp // 2
    c = dp % 2
    n = sec * 8 + dp
    x, y = mp // 4, mp % 4
    u = x * (1 - c) + y * c
    v = y * (1 - c) + x * c

    def at_n(k):
        return (k // 8, k % 8, mp)

    def at_z(zz):
        return (zz // 4, (zz % 4) * 2 + c, mp)

    def at_mp(k):
        return (sec, dp, k)

    def at_uv(uu, vv):
        return (sec, dp, (uu * 4 + vv) * (1 - c) + (vv * 4 + uu) * c)

    sibling = (sec, dp + 1 - 2 * c, mp)

    loads = [
        pltpu.make_async_copy(cache_keys.at[pl.ds(sec * 4, 4)], keys_v, load_sem.at[0]),
        pltpu.make_async_copy(cache_values.at[pl.ds(sec * 4, 4)], values_v, load_sem.at[1]),
        pltpu.make_async_copy(out_weight, weight_v, load_sem.at[2]),
        pltpu.make_async_copy(head_amateur, ha_v, load_sem.at[3]),
        pltpu.make_async_copy(head_expert, he_v, load_sem.at[4]),
    ]

    barrier = pltpu.get_barrier_semaphore()

    def greet(k, carry):
        pl.semaphore_signal(
            barrier, inc=1, device_id=at_mp((mp + k) % 16), device_id_type=MESH
        )
        pl.semaphore_signal(
            barrier, inc=1, device_id=at_n((n + k) % 16), device_id_type=MESH
        )
        return carry

    lax.fori_loop(1, 16, greet, 0)
    for load in loads:
        load.start()

    amateur[c, z, 0:256, :] = hidden_amateur[...]
    row16 = iota((16, 256), 0)
    gains = jnp.where(
        row16 == 0,
        gain_expert[:, 0:256].astype(F32),
        jnp.where(
            row16 == 1,
            gain_expert[:, 256:512].astype(F32),
            jnp.where(row16 == 2, gain_amateur[...].astype(F32), 0.0),
        ),
    )
    amateur[c, z, 256:272, :] = gains.astype(BF16)
    pl.semaphore_wait(barrier, 30)

    def am_copy(way, step):
        if way == 0:
            block, target = (z - step + 9) % 8, (z + 1) % 8
        else:
            block, target = (z + step - 1) % 8, (z + 7) % 8
        ref = amateur.at[c, block]
        return rcopy(ref, ref, am_send.at[way, step], am_recv.at[way, step], at_z(target))

    def am_relay(block):
        ref = amateur.at[c, block]
        return rcopy(ref, ref, am_rsend.at[block], am_rrecv.at[block], sibling)

    def am_advance(step):
        am_copy(0, step).wait_recv()
        if step < 4:
            am_copy(0, step + 1).start()
        am_relay((z - step + 8) % 8).start()
        if step < 4:
            am_copy(1, step).wait_recv()
            if step < 3:
                am_copy(1, step + 1).start()
            am_relay((z + step) % 8).start()

    am_copy(0, 1).start()
    am_copy(1, 1).start()
    am_relay(z).start()

    row_i, col_i = iota((128, 128), 0), iota((128, 128), 1)
    limit = jnp.zeros((128, 128), jnp.int32)
    for r in range(4):
        limit = jnp.where(row_i // 32 == r, lengths[sec * 4 + r], limit)
    live_old = (row_i // 32 == (col_i // 4) % 4) & (row_i % 32 + mp * 32 < limit)
    row_n, col_n = iota((16, 128), 0), iota((16, 128), 1)
    live_new = (row_n // 4 == (col_n // 4) % 4) & (row_n % 4 <= col_n % 4) & (mp == 0)
    loads[0].wait()
    loads[1].wait()

    def stacked(ref, start):
        part = ref[pl.ds(sec * 4, 4), :, pl.ds(start, HD)].astype(F32)
        return jnp.concatenate([part[r] for r in range(4)], axis=0)

    def attend(i, carry):
        g = (mp // 2 + 1 + i) % 8
        base = pl.multiple_of(g * HD, HD)
        keys_old = keys_v[:, :, pl.ds(base, HD)].reshape(128, HD)
        values_old = values_v[:, :, pl.ds(base, HD)].reshape(128, HD)
        keys_new = stacked(new_keys, base).astype(BF16)
        values_new = stacked(new_values, base).astype(BF16)
        query = jnp.concatenate(
            [stacked(queries, pl.multiple_of(g * 1024 + h * HD, HD)) for h in range(8)], axis=0
        ).astype(BF16)
        scaling = 1.0 / HD**0.5
        s_old = lax.dot_general(keys_old, query, NT, preferred_element_type=F32) * scaling
        s_new = lax.dot_general(keys_new, query, NT, preferred_element_type=F32) * scaling
        s_old = jnp.where(live_old, s_old, NEGATIVE)
        s_new = jnp.where(live_new, s_new, NEGATIVE)
        top = jnp.maximum(
            jnp.max(s_old, axis=0, keepdims=True), jnp.max(s_new, axis=0, keepdims=True)
        )
        top = top.astype(BF16).astype(F32)
        p_old = jnp.where(live_old, jnp.exp(s_old - top), 0.0)
        p_new = jnp.where(live_new, jnp.exp(s_new - top), 0.0)
        total = jnp.sum(p_old, axis=0, keepdims=True) + jnp.sum(p_new, axis=0, keepdims=True)
        mix = lax.dot_general(
            p_old.astype(BF16), values_old, TN, preferred_element_type=F32
        ) + lax.dot_general(p_new.astype(BF16), values_new, TN, preferred_element_type=F32)
        high = total.astype(BF16).astype(F32)
        tile = jnp.where(
            row_n == 0,
            top,
            jnp.where(row_n == 1, high, jnp.where(row_n == 2, total - high, 0.0)),
        ).astype(BF16)
        mix = mix.astype(BF16)
        for e in range(2):
            dest = 2 * g + e
            state_out[dest, 0:64, :] = mix[e * 64 : e * 64 + 64]
            state_out[dest, 64:80, :] = tile

            @pl.when(dest != mp)
            def _():
                rcopy(
                    state_out.at[dest],
                    state_in.at[mp],
                    state_sem.at[0],
                    state_sem.at[1],
                    at_mp(dest),
                ).start()

        return carry

    lax.fori_loop(0, 8, attend, 0)
    state_in[mp] = state_out[mp]
    am_advance(1)
    fifteen = pl.ds(0, 15)
    state_all = rcopy(
        state_out.at[fifteen], state_in.at[fifteen], state_sem.at[0], state_sem.at[1], sibling
    )
    state_all.wait_recv()

    tiles = [state_in[k, 64:80, :].astype(F32) for k in range(16)]
    top = tiles[0][0:1]
    for k in range(1, 16):
        top = jnp.maximum(top, tiles[k][0:1])
    total = jnp.zeros((1, 128), F32)
    weights = jnp.zeros((128, 128), F32)
    for k in range(16):
        scale = jnp.exp(tiles[k][0:1] - top)
        total = total + scale * (tiles[k][1:2] + tiles[k][2:3])
        weights = jnp.where(row_i == k, scale, weights)
    scale_t[...] = (weights / total).T
    own = scale_t[pl.ds(pl.multiple_of((mp % 2) * 64, 64), 64), :]
    mixed = jnp.zeros((64, HD), F32)
    for k in range(16):
        mixed = mixed + own[:, k : k + 1] * state_in[k, 0:64, :].astype(F32)

    block = dp * 2 + sec
    attended[block] = mixed.astype(BF16).reshape(4, 16, HD)

    def send_attended(k, carry):
        rcopy(
            attended.at[block],
            attended.at[block],
            attended_sem.at[0],
            attended_sem.at[1],
            at_n((n + k) % 16),
        ).start()
        return carry

    lax.fori_loop(1, 16, send_attended, 0)
    am_advance(2)
    loads[2].wait()
    attended_all = rcopy(
        attended.at[fifteen], attended.at[fifteen], attended_sem.at[0], attended_sem.at[1], sibling
    )
    attended_all.wait_recv()
    partial = jnp.zeros((256, 512), F32)
    for h in range(4):
        partial = partial + jnp.dot(
            attended[:, h].reshape(256, HD),
            weight_v[h * HD : (h + 1) * HD, :],
            preferred_element_type=F32,
        )
    part_out[...] = partial.astype(BF16).reshape(16, 16, 512)

    def send_part(k, carry):
        dest = (mp + k) % 16
        rcopy(
            part_out.at[dest], part_in.at[mp], part_sem.at[0], part_sem.at[1], at_mp(dest)
        ).start()
        return carry

    lax.fori_loop(1, 16, send_part, 0)
    part_in[mp] = part_out[mp]
    am_advance(3)
    part_all = rcopy(
        part_out.at[fifteen], part_in.at[fifteen], part_sem.at[0], part_sem.at[1], sibling
    )
    part_all.wait_recv()
    hidden = resid[pl.ds(pl.multiple_of(mp * 16, 16), 16), :].astype(F32)
    projected = part_in[0].astype(F32)
    for k in range(1, 16):
        projected = projected + part_in[k].astype(F32)
    full[c, z, v, u] = (hidden + projected).astype(BF16)

    def send_one(k, carry):
        rcopy(
            full.at[c, z, v, u], full.at[c, z, v, u], one_sem.at[0], one_sem.at[1], at_z((z + k) % 8)
        ).start()
        return carry

    lax.fori_loop(1, 8, send_one, 0)
    am_advance(4)
    one_all = rcopy(
        full.at[c, pl.ds(0, 7), v, u],
        full.at[c, pl.ds(0, 7), v, u],
        one_sem.at[0],
        one_sem.at[1],
        sibling,
    )
    one_all.wait_recv()

    def send_two(k, carry):
        rcopy(
            full.at[c, :, v, u],
            full.at[c, :, v, u],
            two_sem.at[0],
            two_sem.at[1],
            at_uv((u + k) % 4, v),
        ).start()
        return carry

    lax.fori_loop(1, 4, send_two, 0)

    loads[3].wait()
    acc_a[...] = jnp.zeros_like(acc_a)
    acc_e[...] = jnp.zeros_like(acc_e)
    square_a[...] = jnp.zeros_like(square_a)
    square_e[...] = jnp.zeros_like(square_e)
    other = rcopy(amateur.at[c, 0], amateur.at[c, 0], am_rsend.at[0], am_rrecv.at[0], sibling)

    def am_block(k, carry):
        ref = amateur.at[1 - c, k]
        rcopy(ref, ref, am_rsend.at[k], am_rrecv.at[k], sibling).wait_recv()
        parts = []
        squares = square_a[...]
        for cc in range(2):
            wide = amateur[cc, k, 0:256, :].astype(F32)
            gain = amateur[cc, k, 256:272, :].astype(F32)[2:3]
            squares = squares + wide[:, 0:128] * wide[:, 0:128] + wide[:, 128:] * wide[:, 128:]
            parts.append((wide * gain).astype(BF16))
        square_a[...] = squares
        acc_a[...] += lax.dot_general(
            ha_v[:, pl.ds(pl.multiple_of(k * 512, 512), 512)],
            jnp.concatenate(parts, axis=1),
            NT,
            preferred_element_type=F32,
        )
        return carry

    lax.fori_loop(0, 8, am_block, 0)
    ones = jnp.ones((8, 128), F32)

    def inverse_norm(ref, width):
        sums = lax.dot_general(
            ones, ref[...], NT, preferred_element_type=F32, precision=lax.Precision.HIGHEST
        )
        return lax.rsqrt(sums[0:1] / width + EPSILON)

    logits_a = acc_a[...] * inverse_norm(square_a, 4096.0)
    acc_a[...] = logits_a
    top_a = jnp.max(logits_a, axis=0, keepdims=True)
    total_a = jnp.sum(jnp.exp(logits_a - top_a), axis=0, keepdims=True)

    two_all = rcopy(
        full.at[c, :, v, pl.ds(0, 3)],
        full.at[c, :, v, pl.ds(0, 3)],
        two_sem.at[0],
        two_sem.at[1],
        sibling,
    )
    two_all.wait_recv()
    above, below = (v + 1) % 4, (v + 3) % 4

    def three(which, zz, vv, target):
        ref = full.at[c, zz, vv]
        return rcopy(
            ref, ref, three_send.at[which, zz], three_recv.at[which, zz], at_uv(u, target)
        )

    def send_three(zz):
        three(0, zz, v, above).start()
        three(1, zz, v, below).start()

    def relay(zz, cc):
        ref = full.at[cc, zz]
        return rcopy(ref, ref, relay_send.at[zz], relay_recv.at[zz], sibling)

    send_three(0)
    send_three(1)
    loads[4].wait()

    def gather_block(zz, carry):
        @pl.when(zz < 6)
        def _():
            send_three(zz + 2)

        @pl.when(zz < 8)
        def _():
            three(0, zz, below, above).wait_recv()
            three(1, zz, above, below).wait_recv()

            @pl.when(zz % 2 == 0)
            def _():
                three(2, zz, below, above).start()

            @pl.when(zz % 2 == 1)
            def _():
                three(2, zz, above, below).start()

        @pl.when((zz >= 1) & (zz < 9))
        def _():
            three(2, zz - 1, (v + 2) % 4, above).wait_recv()
            relay(zz - 1, c).start()

        @pl.when(zz >= 2)
        def _():
            k = zz - 2
            relay(k, 1 - c).wait_recv()
            parts = []
            squares = square_e[...]
            for cc in range(2):
                wide = full[cc, k]
                if cc == 0:
                    wide = jnp.swapaxes(wide, 0, 1)
                wide = wide.reshape(256, 512).astype(F32)
                tile = amateur[cc, k, 256:272, :].astype(F32)
                for half in range(2):
                    piece = wide[:, half * 256 : half * 256 + 256]
                    squares = (
                        squares
                        + piece[:, 0:128] * piece[:, 0:128]
                        + piece[:, 128:] * piece[:, 128:]
                    )
                    parts.append((piece * tile[half : half + 1]).astype(BF16))
            square_e[...] = squares
            acc_e[...] += lax.dot_general(
                he_v[:, pl.ds(pl.multiple_of(k * 1024, 1024), 1024)],
                jnp.concatenate(parts, axis=1),
                NT,
                preferred_element_type=F32,
            )

        return carry

    lax.fori_loop(0, 10, gather_block, 0)

    logits_e = acc_e[...] * inverse_norm(square_e, 8192.0)
    top_e = jnp.max(logits_e, axis=0, keepdims=True)
    total_e = jnp.sum(jnp.exp(logits_e - top_e), axis=0, keepdims=True)
    difference = logits_e - CONTRAST * acc_a[...]
    pick_row = (iota((64, 256), 1) // 4 == iota((64, 256), 0)).astype(F32)
    step_row = iota((8, 256), 1) % 4 == iota((8, 256), 0)
    spread = jnp.dot(
        chosen[...].astype(F32),
        pick_row,
        preferred_element_type=F32,
        precision=lax.Precision.HIGHEST,
    )
    target = jnp.sum(jnp.where(step_row[0:4], spread, 0.0), axis=0, keepdims=True)
    target = target - ((n * 16 + mp) * 512).astype(F32)
    matched = iota((512, 256), 0).astype(F32) == target
    picked = jnp.sum(jnp.where(matched, difference, 0.0), axis=0, keepdims=True)

    row8 = iota((8, 256), 0)

    def pack(rows):
        tile = jnp.zeros((8, 256), F32)
        for k, row in enumerate(rows):
            tile = jnp.where(row8 == k, row, tile)
        return tile

    def join(ref):
        tiles = [ref[k] for k in range(16)]
        top = tiles[0]
        for k in range(1, 16):
            top = jnp.maximum(top, tiles[k])
        te, ta = top[0:1], top[2:3]
        se, sa, pick = jnp.zeros((1, 256), F32), jnp.zeros((1, 256), F32), jnp.zeros((1, 256), F32)
        for k in range(16):
            se = se + tiles[k][1:2] * jnp.exp(tiles[k][0:1] - te)
            sa = sa + tiles[k][3:4] * jnp.exp(tiles[k][2:3] - ta)
            pick = pick + tiles[k][4:5]
        return te, se, ta, sa, pick

    stats_p[mp] = pack((top_e, total_e, top_a, total_a, picked))

    def send_p(k, carry):
        rcopy(
            stats_p.at[mp], stats_p.at[mp], stats_sem.at[0], stats_sem.at[1], at_mp((mp + k) % 16)
        ).start()
        return carry

    lax.fori_loop(1, 16, send_p, 0)
    diff[...] = difference.T
    p_all = rcopy(
        stats_p.at[fifteen], stats_p.at[fifteen], stats_sem.at[0], stats_sem.at[1], sibling
    )
    p_all.wait_recv()
    stats_z[n] = pack(join(stats_p))

    def send_z(k, carry):
        rcopy(
            stats_z.at[n], stats_z.at[n], stats_sem.at[2], stats_sem.at[3], at_n((n + k) % 16)
        ).start()
        return carry

    lax.fori_loop(1, 16, send_z, 0)

    state_all.wait_send()
    attended_all.wait_send()
    part_all.wait_send()
    one_all.wait_send()
    two_all.wait_send()
    p_all.wait_send()
    for step in range(1, 5):
        am_copy(0, step).wait_send()
        if step < 4:
            am_copy(1, step).wait_send()

    def drain(k, carry):
        relay(k, c).wait_send()
        am_relay(k).wait_send()
        for which in range(3):
            three(which, k, v, above).wait_send()
        return carry

    lax.fori_loop(0, 8, drain, 0)
    z_all = rcopy(
        stats_z.at[fifteen], stats_z.at[fifteen], stats_sem.at[2], stats_sem.at[3], sibling
    )
    z_all.wait_recv()
    te, se, ta, sa, pick = join(stats_z)
    shift = te + jnp.log(se) - CONTRAST * (ta + jnp.log(sa))
    shift_t = jnp.where(iota((128, 256), 0) == 0, shift, 0.0).T
    out[...] = (diff[...] - shift_t[:, 0:1]).astype(BF16)
    masked = jnp.where(step_row, pick - shift, 0.0)
    out_chosen[...] = lax.dot_general(
        masked, pick_row, NT, preferred_element_type=F32, precision=lax.Precision.HIGHEST
    )[0:4]
    z_all.wait_send()


def local(
    queries,
    new_keys,
    new_values,
    cache_keys,
    cache_values,
    lengths,
    out_weight,
    resid_expert,
    gain_expert,
    hidden_amateur,
    gain_amateur,
    head_expert,
    head_amateur,
    chosen,
):
    vmem = pl.BlockSpec(memory_space=pltpu.VMEM)
    hbm = pl.BlockSpec(memory_space=pl.ANY)
    dma = pltpu.SemaphoreType.DMA
    scores, chosen_score = pl.pallas_call(
        kernel,
        out_shape=(
            jax.ShapeDtypeStruct((256, 512), BF16),
            jax.ShapeDtypeStruct((4, 64), F32),
        ),
        in_specs=[pl.BlockSpec(memory_space=pltpu.SMEM)] + [vmem] * 8 + [hbm] * 5,
        out_specs=(vmem, vmem),
        scratch_shapes=[
            pltpu.VMEM((4, 32, 1024), BF16),
            pltpu.VMEM((4, 32, 1024), BF16),
            pltpu.VMEM((512, 512), BF16),
            pltpu.VMEM((512, 8192), BF16),
            pltpu.VMEM((512, 4096), BF16),
            pltpu.VMEM((16, 80, 128), BF16),
            pltpu.VMEM((16, 80, 128), BF16),
            pltpu.VMEM((128, 128), F32),
            pltpu.VMEM((16, 4, 16, 128), BF16),
            pltpu.VMEM((16, 16, 512), BF16),
            pltpu.VMEM((16, 16, 512), BF16),
            pltpu.VMEM((2, 8, 4, 4, 16, 512), BF16),
            pltpu.VMEM((2, 8, 272, 256), BF16),
            pltpu.VMEM((512, 256), F32),
            pltpu.VMEM((512, 256), F32),
            pltpu.VMEM((256, 128), F32),
            pltpu.VMEM((256, 128), F32),
            pltpu.VMEM((256, 512), F32),
            pltpu.VMEM((16, 8, 256), F32),
            pltpu.VMEM((16, 8, 256), F32),
            dma((5,)),
            dma((2,)),
            dma((2,)),
            dma((2,)),
            dma((2,)),
            dma((2,)),
            dma((3, 8)),
            dma((3, 8)),
            dma((8,)),
            dma((8,)),
            dma((2, 5)),
            dma((2, 5)),
            dma((8,)),
            dma((8,)),
            dma((4,)),
        ],
        compiler_params=pltpu.CompilerParams(
            collective_id=0, has_side_effects=True, vmem_limit_bytes=56 * 1024 * 1024
        ),
        name="contrast",
    )(
        lengths,
        queries,
        new_keys,
        new_values,
        resid_expert,
        gain_expert.reshape(1, -1),
        gain_amateur.reshape(1, -1),
        hidden_amateur,
        chosen.T,
        cache_keys,
        cache_values,
        out_weight,
        head_expert,
        head_amateur,
    )
    return scores.reshape(64, 4, 512), chosen_score.T


def solution(mesh):
    return jax.shard_map(
        local,
        mesh=mesh,
        in_specs=(
            P("dp", None, None),
            P("dp", None, None),
            P("dp", None, None),
            P("dp", "mp", None),
            P("dp", "mp", None),
            P("dp"),
            P("mp", ("section", "dp")),
            P(None, ("section", "dp")),
            P(("section", "dp")),
            P(None, ("section", "dp")),
            P(("section", "dp")),
            P(("section", "dp", "mp"), None),
            P(("section", "dp", "mp"), None),
            P(),
        ),
        out_specs=(P(None, None, ("section", "dp", "mp")), P()),
        check_vma=False,
    )
```

time: 887 us -> 92.2 us (0.10)
  blocking collectives: 595 us -> 0 us
  waiting for transfers between devices: 173 us -> 0 us
  Pallas kernels: 0 us -> 85.9 us
  other arithmetic: 55.5 us -> 0 us
  matrix products: 16.1 us -> 0 us
  between operations: 16 us -> 0.64 us
  local copies, waits for them, and re-layouts: 18.4 us -> 5.44 us
  loops' own time: 12.4 us -> 0 us
    all_gather x10 -> x0, blocking collectives: 595 us -> none  [the longest x7 545 us: merged(): everything = jax.tree.map(lambda part: lax.all_gather(part, axis), array)]
    psum x1 -> x0, waiting for transfers between devices: 92.6 us -> none  [local(): projected = lax.psum(partial_sum, 'mp')]
    pallas_call x0 -> x1, Pallas kernels: none -> 85.9 us  [local(): pl.pallas_call(kernel, out_shape=(jax.ShapeDtypeStruct((256, 512), BF16),...]
    all_gather x3 -> x0, waiting for transfers between devices: 79.9 us -> none  [the longest x1 79.8 us: merged(): everything = jax.tree.map(lambda part: lax.all_gather(part, axis), array)]
    add x798 -> x0, other arithmetic: 46.1 us -> none  [the longest x15 32.8 us: join_heads(): first_part[2] * first_scale[..., None]]
    dot_general x7 -> x0, matrix products: 16.1 us -> none  [the longest x1 5.85 us: local(): lax.dot_general(normed_expert, head_expert, (((1,), (1,)), ((), ())), pre...]
    another operation x2 -> x0, loops' own time: 12.4 us -> none  [merged(): return lax.fori_loop(1, lax.axis_size(axis), hop, initial)]
    dynamic_slice x781 -> x0, local copies, waits for them, and re-layouts: 9.62 us -> none  [the longest x780 9.54 us: hop(): return combine(so_far, jax.tree.map(lambda part: part[k], everything))]
  transfers between devices with their start and end apart: 4 -> 0, of which waited for: 2 -> 0; matrix products, arithmetic and copies ran while one was open for 1% -> 0% of each run, Pallas kernels for 0% -> 0%
where the time goes in v1:
time: 92.2 us; the launch traced here: 92 us
  Pallas kernels  85.9 us (93%)
  local copies, waits for them, and re-layouts  5.44 us (6%)
    pallas_call x1, Pallas kernels, local(): pl.pallas_call(kernel, out_shape=(jax.ShapeDtypeStruct((256, 512), BF16),...  85.9 us

profile of v1, /device:TPU:1, one launch (start us, length us, event | category | flops | bytes accessed | tf_op | source)
XLA Modules:
  0.0 92.0 jit_solution(13726188522808317050)
XLA Ops:
  0.6 1.2 %reshape.14.gain_amateur = bf16[1,256]{1,0:T(2,128)(2,1)} reshape(bf16[256]{0:T(256)(128)(2,1)} %param.24) | data formatting | bytes 1024 | tf_op jit(solution)/shard_map/reshape | solution.py:636
  1.8 1.3 %reshape.13.gain_expert = bf16[1,512]{1,0:T(2,128)(2,1)} reshape(bf16[512]{0:T(512)(128)(2,1)} %param.22) | data formatting | bytes 2048 | tf_op jit(solution)/shard_map/reshape | solution.py:635
  3.1 85.9 %contrast.1 = (bf16[256,512]{1,0:T(8,128)(2,1)}, f32[4,64]{1,0:T(4,128)}) custom-call(s32[8]{0:T(128)} %lengths.1, bf16[8,4,8192]{2,1,0:T(4,128)(2,1)} %queries.1, bf16[8,4,1024]{2,1,0:T(4,128)(2,1)} %new_keys.1, bf16[8,4,1024]{2,1,0:T(4,128)(2,1)} %new_values.1, bf16[256,512]{1,0:T(8,128)(2,1)} %resid.1, bf16[1,512]{1,0:T(2,128)(2,1)} %reshape.13.gain_expert, ...), custom_call_target="tpu_custom_call" | custom-call | tf_op jit(solution)/shard_map/contrast/pallas_call | solution.py:580
  89.0 1.7 %reshape.15 = bf16[64,4,512]{2,1,0:T(4,128)(2,1)} reshape(bf16[256,512]{1,0:T(8,128)(2,1)} %get-tuple-element.4) | data formatting | bytes 524288 | tf_op jit(solution)/shard_map/reshape | solution.py:645
  90.8 1.2 %copy.17 = f32[64,4]{0,1:T(4,128)} copy(f32[64,4]{0,1:T(4,128)} %bitcast.2) | data formatting | bytes 2048

commit v2 on v1

v2 whole, which is shorter than its diff:
```python
import jax
import jax.numpy as jnp
from jax import lax
from jax.experimental import pallas as pl
from jax.experimental.pallas import tpu as pltpu
from jax.sharding import PartitionSpec as P

MESH = pl.DeviceIdType.MESH
F32 = jnp.float32
BF16 = jnp.bfloat16
KVH = 8
HD = 128
CONTRAST = 0.5
NEGATIVE = -1e30
EPSILON = 1e-05
NT = (((1,), (1,)), ((), ()))
TN = (((0,), (0,)), ((), ()))


def rcopy(src, dst, send_sem, recv_sem, device):
    return pltpu.make_async_remote_copy(
        src_ref=src,
        dst_ref=dst,
        send_sem=send_sem,
        recv_sem=recv_sem,
        device_id=device,
        device_id_type=MESH,
    )


def iota(shape, dim):
    return lax.broadcasted_iota(jnp.int32, shape, dim)


def kernel(
    lengths,
    queries,
    new_keys,
    new_values,
    resid,
    gain_expert,
    gain_amateur,
    hidden_amateur,
    chosen,
    cache_keys,
    cache_values,
    out_weight,
    head_expert,
    head_amateur,
    out,
    out_chosen,
    keys_v,
    values_v,
    weight_v,
    he_v,
    ha_v,
    state_out,
    state_in,
    scale_t,
    attended,
    part_out,
    part_in,
    full,
    amateur,
    acc_e,
    acc_a,
    square_e,
    square_a,
    diff,
    stats_s,
    stats_h,
    stats_p,
    stats_z,
    stats_f,
    load_sem,
    state_sem,
    attended_sem,
    part_sem,
    one_send,
    one_recv,
    two_send,
    two_recv,
    three_send,
    three_recv,
    relay_send,
    relay_recv,
    am_send,
    am_recv,
    stats_send,
    stats_recv,
):
    sec = lax.axis_index("section")
    dp = lax.axis_index("dp")
    mp = lax.axis_index("mp")
    z = sec * 4 + dp // 2
    c = dp % 2
    n = sec * 8 + dp
    x, y = mp // 4, mp % 4
    u = x * (1 - c) + y * c
    v = y * (1 - c) + x * c

    def at_n(k):
        return (k // 8, k % 8, mp)

    def at_z(zz):
        return (zz // 4, (zz % 4) * 2 + c, mp)

    def at_mp(k):
        return (sec, dp, k)

    def at_uv(uu, vv):
        return (sec, dp, (uu * 4 + vv) * (1 - c) + (vv * 4 + uu) * c)

    sibling = (sec, dp + 1 - 2 * c, mp)

    loads = [
        pltpu.make_async_copy(cache_keys.at[pl.ds(sec * 4, 4)], keys_v, load_sem.at[0]),
        pltpu.make_async_copy(cache_values.at[pl.ds(sec * 4, 4)], values_v, load_sem.at[1]),
        pltpu.make_async_copy(out_weight, weight_v, load_sem.at[2]),
        pltpu.make_async_copy(head_amateur, ha_v, load_sem.at[3]),
        pltpu.make_async_copy(head_expert, he_v, load_sem.at[4]),
    ]

    barrier = pltpu.get_barrier_semaphore()

    def greet_mp(k, carry):
        pl.semaphore_signal(
            barrier, inc=1, device_id=at_mp((mp + k) % 16), device_id_type=MESH
        )
        return carry

    def greet_z(k, carry):
        pl.semaphore_signal(
            barrier, inc=1, device_id=at_z((z + k) % 8), device_id_type=MESH
        )
        return carry

    lax.fori_loop(1, 8, greet_z, 0)
    lax.fori_loop(1, 16, greet_mp, 0)
    pl.semaphore_signal(barrier, inc=1, device_id=sibling, device_id_type=MESH)
    for load in loads:
        load.start()

    amateur[c, z, u, 0:64, :] = hidden_amateur[pl.ds(pl.multiple_of(u * 64, 64), 64), :]
    row16 = iota((16, 256), 0)
    gains = jnp.where(
        row16 == 0,
        gain_expert[0:256].astype(F32).reshape(1, 256),
        jnp.where(
            row16 == 1,
            gain_expert[256:512].astype(F32).reshape(1, 256),
            jnp.where(row16 == 2, gain_amateur[...].astype(F32).reshape(1, 256), 0.0),
        ),
    )
    amateur[c, z, u, 64:80, :] = gains.astype(BF16)

    row_i, col_i = iota((128, 128), 0), iota((128, 128), 1)
    limit = jnp.zeros((128, 128), jnp.int32)
    for r in range(4):
        limit = jnp.where(row_i // 32 == r, lengths[sec * 4 + r], limit)
    live_old = (row_i // 32 == (col_i // 4) % 4) & (row_i % 32 + mp * 32 < limit)
    row_n, col_n = iota((16, 128), 0), iota((16, 128), 1)
    live_new = (row_n // 4 == (col_n // 4) % 4) & (row_n % 4 <= col_n % 4) & (mp == 0)
    loads[0].wait()
    loads[1].wait()

    def stacked(ref, start):
        part = ref[pl.ds(sec * 4, 4), :, pl.ds(start, HD)].astype(F32)
        return jnp.concatenate([part[r] for r in range(4)], axis=0)

    def attend(i, carry):
        g = i
        base = pl.multiple_of(g * HD, HD)
        keys_old = keys_v[:, :, pl.ds(base, HD)].reshape(128, HD)
        values_old = values_v[:, :, pl.ds(base, HD)].reshape(128, HD)
        keys_new = stacked(new_keys, base).astype(BF16)
        values_new = stacked(new_values, base).astype(BF16)
        query = jnp.concatenate(
            [stacked(queries, pl.multiple_of(g * 1024 + h * HD, HD)) for h in range(8)], axis=0
        ).astype(BF16)
        scaling = 1.0 / HD**0.5
        s_old = lax.dot_general(keys_old, query, NT, preferred_element_type=F32) * scaling
        s_new = lax.dot_general(keys_new, query, NT, preferred_element_type=F32) * scaling
        s_old = jnp.where(live_old, s_old, NEGATIVE)
        s_new = jnp.where(live_new, s_new, NEGATIVE)
        top = jnp.maximum(
            jnp.max(s_old, axis=0, keepdims=True), jnp.max(s_new, axis=0, keepdims=True)
        )
        top = top.astype(BF16).astype(F32)
        p_old = jnp.where(live_old, jnp.exp(s_old - top), 0.0)
        p_new = jnp.where(live_new, jnp.exp(s_new - top), 0.0)
        total = jnp.sum(p_old, axis=0, keepdims=True) + jnp.sum(p_new, axis=0, keepdims=True)
        mix = lax.dot_general(
            p_old.astype(BF16), values_old, TN, preferred_element_type=F32
        ) + lax.dot_general(p_new.astype(BF16), values_new, TN, preferred_element_type=F32)
        high = total.astype(BF16).astype(F32)
        tile = jnp.where(
            row_n == 0,
            top,
            jnp.where(row_n == 1, high, jnp.where(row_n == 2, total - high, 0.0)),
        ).astype(BF16)
        mix = mix.astype(BF16)
        for e in range(2):
            state_out[2 * g + e, 0:64, :] = mix[e * 64 : e * 64 + 64]
            state_out[2 * g + e, 64:80, :] = tile
        return carry

    lax.fori_loop(0, 8, attend, 0)
    pl.semaphore_wait(barrier, 23)

    def send_state(k, carry):
        dest = (mp + k) % 16
        rcopy(
            state_out.at[dest], state_in.at[mp], state_sem.at[0], state_sem.at[1], at_mp(dest)
        ).start()
        return carry

    lax.fori_loop(1, 16, send_state, 0)

    def send_am(k, carry):
        ref = amateur.at[c, z, u]
        rcopy(ref, ref, am_send.at[0], am_recv.at[0], at_z((z + k) % 8)).start()
        return carry

    lax.fori_loop(1, 8, send_am, 0)
    state_in[mp] = state_out[mp]
    fifteen = pl.ds(0, 15)
    state_all = rcopy(
        state_out.at[fifteen], state_in.at[fifteen], state_sem.at[0], state_sem.at[1], sibling
    )
    state_all.wait_recv()

    tiles = [state_in[k, 64:80, :].astype(F32) for k in range(16)]
    top = tiles[0][0:1]
    for k in range(1, 16):
        top = jnp.maximum(top, tiles[k][0:1])
    total = jnp.zeros((1, 128), F32)
    weights = jnp.zeros((128, 128), F32)
    for k in range(16):
        scale = jnp.exp(tiles[k][0:1] - top)
        total = total + scale * (tiles[k][1:2] + tiles[k][2:3])
        weights = jnp.where(row_i == k, scale, weights)
    scale_t[...] = (weights / total).T
    own = scale_t[pl.ds(pl.multiple_of((mp % 2) * 64, 64), 64), :]
    mixed = jnp.zeros((64, HD), F32)
    for k in range(16):
        mixed = mixed + own[:, k : k + 1] * state_in[k, 0:64, :].astype(F32)

    attended[c, z] = mixed.astype(BF16).reshape(4, 16, HD)

    def send_attended(k, carry):
        ref = attended.at[c, z]
        rcopy(ref, ref, attended_sem.at[0], attended_sem.at[1], at_z((z + k) % 8)).start()
        return carry

    lax.fori_loop(1, 8, send_attended, 0)

    am_one = amateur.at[c, pl.ds(0, 7), u]
    am_first = rcopy(am_one, am_one, am_send.at[0], am_recv.at[0], sibling)
    am_first.wait_recv()

    def send_quarter(k, carry):
        ref = amateur.at[c, :, u, pl.ds(0, 64)]
        rcopy(ref, ref, am_send.at[1], am_recv.at[1], at_uv((u + k) % 4, v)).start()
        return carry

    lax.fori_loop(1, 4, send_quarter, 0)
    loads[2].wait()
    seven = attended.at[c, pl.ds(0, 7)]
    attended_all = rcopy(seven, seven, attended_sem.at[0], attended_sem.at[1], sibling)
    attended_all.wait_recv()

    def pass_attended(cc):
        ref = attended.at[cc]
        return rcopy(ref, ref, attended_sem.at[2], attended_sem.at[3], sibling)

    pass_attended(c).start()

    def project(cc):
        partial = jnp.zeros((128, 512), F32)
        for h in range(4):
            partial = partial + jnp.dot(
                attended[cc, :, h].reshape(128, HD),
                weight_v[h * HD : (h + 1) * HD, :],
                preferred_element_type=F32,
            )
        part_out[cc] = partial.astype(BF16).reshape(8, 16, 512)

        def send_part(zz, carry):
            dest = (zz % 4) * 4 + cc * 2 + zz // 4

            @pl.when(dest != mp)
            def _():
                rcopy(
                    part_out.at[cc, zz], part_in.at[mp], part_sem.at[0], part_sem.at[1], at_mp(dest)
                ).start()

            return carry

        lax.fori_loop(0, 8, send_part, 0)

    project(c)
    pass_attended(1 - c).wait_recv()
    project(1 - c)
    part_in[mp] = part_out[(mp // 2) % 2, (mp % 2) * 4 + mp // 4]

    am_two = amateur.at[c, :, pl.ds(0, 3), pl.ds(0, 64)]
    am_second = rcopy(am_two, am_two, am_send.at[1], am_recv.at[1], sibling)
    am_second.wait_recv()

    def am_pass(cc):
        ref = amateur.at[cc]
        return rcopy(ref, ref, am_send.at[2], am_recv.at[2], sibling)

    am_pass(c).start()
    part_all = rcopy(
        part_in.at[fifteen], part_in.at[fifteen], part_sem.at[0], part_sem.at[1], sibling
    )
    part_all.wait_recv()
    hidden = resid[pl.ds(pl.multiple_of(mp * 16, 16), 16), :].astype(F32)
    projected = part_in[0].astype(F32)
    for k in range(1, 16):
        projected = projected + part_in[k].astype(F32)
    full[c, z, v, u] = (hidden + projected).astype(BF16)

    def one(block, target):
        ref = full.at[c, block, v, u]
        return rcopy(ref, ref, one_send, one_recv.at[block], at_z(target))

    def send_one(k, carry):
        one(z, (z + k) % 8).start()
        return carry

    lax.fori_loop(1, 8, send_one, 0)

    def two(half, k):
        ref = full.at[c, pl.ds(half * 4, 4), v, u]
        return rcopy(
            ref, ref, two_send.at[half], two_recv.at[half], at_uv((u + k) % 4, v)
        )

    def three(k, zz, vv):
        ref = full.at[c, zz, vv]
        return rcopy(
            ref, ref, three_send.at[zz], three_recv.at[k, zz], at_uv(u, (v + k) % 4)
        )

    def relay(zz, cc):
        ref = full.at[cc, zz]
        return rcopy(ref, ref, relay_send.at[zz], relay_recv.at[zz], sibling)

    for half in range(2):

        def wait_one(zz, carry):
            @pl.when(zz != z)
            def _():
                one(zz, z).wait_recv()

            return carry

        lax.fori_loop(half * 4, half * 4 + 4, wait_one, 0)
        for k in range(1, 4):
            two(half, k).start()

    def two_all(half):
        ref = full.at[c, pl.ds(half * 4, 4), v, pl.ds(0, 3)]
        return rcopy(ref, ref, two_send.at[half], two_recv.at[half], sibling)

    for half in range(2):
        two_all(half).wait_recv()

        def send_three(zz, carry):
            for k in (2, 1, 3):
                three(k, zz, v).start()
            return carry

        lax.fori_loop(half * 4, half * 4 + 4, send_three, 0)

    loads[3].wait()
    acc_a[...] = jnp.zeros_like(acc_a)
    acc_e[...] = jnp.zeros_like(acc_e)
    square_a[...] = jnp.zeros_like(square_a)
    square_e[...] = jnp.zeros_like(square_e)
    am_pass(1 - c).wait_recv()

    def am_block(k, carry):
        parts = []
        squares = square_a[...]
        for cc in range(2):
            wide = amateur[cc, k, :, 0:64, :].reshape(256, 256).astype(F32)
            gain = amateur[cc, k, x if cc == 0 else y, 64:80, :].astype(F32)[2:3]
            squares = squares + wide[:, 0:128] * wide[:, 0:128] + wide[:, 128:] * wide[:, 128:]
            parts.append((wide * gain).astype(BF16))
        square_a[...] = squares
        acc_a[...] += lax.dot_general(
            ha_v[:, pl.ds(pl.multiple_of(k * 512, 512), 512)],
            jnp.concatenate(parts, axis=1),
            NT,
            preferred_element_type=F32,
        )
        return carry

    lax.fori_loop(0, 8, am_block, 0)
    ones = jnp.ones((8, 128), F32)

    def inverse_norm(ref, width):
        sums = lax.dot_general(
            ones, ref[...], NT, preferred_element_type=F32, precision=lax.Precision.HIGHEST
        )
        return lax.rsqrt(sums[0:1] / width + EPSILON)

    logits_a = acc_a[...] * inverse_norm(square_a, 4096.0)
    acc_a[...] = logits_a
    top_a = jnp.max(logits_a, axis=0, keepdims=True)
    total_a = jnp.sum(jnp.exp(logits_a - top_a), axis=0, keepdims=True)

    loads[4].wait()

    def gather_block(zz, carry):
        @pl.when(zz < 8)
        def _():
            for k in (1, 3, 2):
                three(k, zz, (v - k + 4) % 4).wait_recv()
            relay(zz, c).start()

        @pl.when(zz >= 1)
        def _():
            k = zz - 1
            relay(k, 1 - c).wait_recv()
            parts = []
            squares = square_e[...]
            for cc in range(2):
                wide = full[cc, k]
                if cc == 0:
                    wide = jnp.swapaxes(wide, 0, 1)
                wide = wide.reshape(256, 512).astype(F32)
                tile = amateur[cc, k, x if cc == 0 else y, 64:80, :].astype(F32)
                for half in range(2):
                    piece = wide[:, half * 256 : half * 256 + 256]
                    squares = (
                        squares
                        + piece[:, 0:128] * piece[:, 0:128]
                        + piece[:, 128:] * piece[:, 128:]
                    )
                    parts.append((piece * tile[half : half + 1]).astype(BF16))
            square_e[...] = squares
            acc_e[...] += lax.dot_general(
                he_v[:, pl.ds(pl.multiple_of(k * 1024, 1024), 1024)],
                jnp.concatenate(parts, axis=1),
                NT,
                preferred_element_type=F32,
            )

        return carry

    lax.fori_loop(0, 9, gather_block, 0)

    logits_e = acc_e[...] * inverse_norm(square_e, 8192.0)
    top_e = jnp.max(logits_e, axis=0, keepdims=True)
    total_e = jnp.sum(jnp.exp(logits_e - top_e), axis=0, keepdims=True)
    difference = logits_e - CONTRAST * acc_a[...]
    pick_row = (iota((64, 256), 1) // 4 == iota((64, 256), 0)).astype(F32)
    step_row = iota((8, 256), 1) % 4 == iota((8, 256), 0)
    spread = jnp.dot(
        chosen[...].astype(F32),
        pick_row,
        preferred_element_type=F32,
        precision=lax.Precision.HIGHEST,
    )
    target = jnp.sum(jnp.where(step_row[0:4], spread, 0.0), axis=0, keepdims=True)
    target = target - ((n * 16 + mp) * 512).astype(F32)
    matched = iota((512, 256), 0).astype(F32) == target
    picked = jnp.sum(jnp.where(matched, difference, 0.0), axis=0, keepdims=True)

    row8 = iota((8, 128), 0)

    def pack(rows, half):
        tile = jnp.zeros((8, 128), F32)
        for k, row in enumerate(rows):
            tile = jnp.where(row8 == k, row[:, half * 128 : half * 128 + 128], tile)
        return tile

    def join(tiles):
        top = tiles[0]
        for tile in tiles[1:]:
            top = jnp.maximum(top, tile)
        te, ta = top[0:1], top[2:3]
        zero = jnp.zeros((1, 128), F32)
        se, sa, pick = zero, zero, zero
        for tile in tiles:
            se = se + tile[1:2] * jnp.exp(tile[0:1] - te)
            sa = sa + tile[3:4] * jnp.exp(tile[2:3] - ta)
            pick = pick + tile[4:5]
        return te, se, ta, sa, pick

    mine = (top_e, total_e, top_a, total_a, picked)
    stats_h[0] = pack(mine, 0)
    stats_h[1] = pack(mine, 1)
    pair = rcopy(stats_h.at[1 - c], stats_s, stats_send.at[0], stats_recv.at[0], sibling)
    pair.start()
    pair.wait_recv()
    stats_p[mp] = pack(join([stats_h[c], stats_s[...]]), 0)

    def send_p(k, carry):
        ref = stats_p.at[mp]
        rcopy(ref, ref, stats_send.at[1], stats_recv.at[1], at_mp((mp + k) % 16)).start()
        return carry

    lax.fori_loop(1, 16, send_p, 0)
    diff[...] = difference.T

    state_all.wait_send()
    attended_all.wait_send()
    pass_attended(c).wait_send()
    am_first.wait_send()
    am_second.wait_send()
    am_pass(c).wait_send()
    part_all.wait_send()
    ref = full.at[c, pl.ds(0, 7), v, u]
    rcopy(ref, ref, one_send, one_recv.at[0], sibling).wait_send()
    for half in range(2):
        two_all(half).wait_send()

    def drain(k, carry):
        relay(k, c).wait_send()
        ref = full.at[c, k, pl.ds(0, 3)]
        rcopy(ref, ref, three_send.at[k], three_recv.at[1, k], sibling).wait_send()
        return carry

    lax.fori_loop(0, 8, drain, 0)
    pair.wait_send()
    ref = stats_p.at[fifteen]
    p_all = rcopy(ref, ref, stats_send.at[1], stats_recv.at[1], sibling)
    p_all.wait_recv()
    stats_z[z] = pack(join([stats_p[k] for k in range(16)]), 0)

    def send_z(k, carry):
        ref = stats_z.at[z]
        rcopy(ref, ref, stats_send.at[2], stats_recv.at[2], at_z((z + k) % 8)).start()
        return carry

    lax.fori_loop(1, 8, send_z, 0)
    p_all.wait_send()
    ref = stats_z.at[pl.ds(0, 7)]
    z_all = rcopy(ref, ref, stats_send.at[2], stats_recv.at[2], sibling)
    z_all.wait_recv()
    te, se, ta, sa, pick = join([stats_z[k] for k in range(8)])
    shift = te + jnp.log(se) - CONTRAST * (ta + jnp.log(sa))
    stats_f[c] = pack((shift, pick - shift), 0)
    last = rcopy(stats_f.at[c], stats_f.at[c], stats_send.at[3], stats_recv.at[3], sibling)
    last.start()
    z_all.wait_send()
    last.wait_recv()
    both = jnp.concatenate([stats_f[0], stats_f[1]], axis=1)
    shift_t = jnp.concatenate([both] * 16, axis=0).T
    out[...] = (diff[...] - shift_t[:, 0:1]).reshape(64, 4, 512).astype(BF16)
    masked = jnp.where(step_row, both[1:2], 0.0)
    out_chosen[...] = lax.dot_general(
        masked, pick_row, NT, preferred_element_type=F32, precision=lax.Precision.HIGHEST
    )[0:4]
    last.wait_send()


def finish(scores, chosen_score, out, out_chosen):
    out[...] = scores[...]
    out_chosen[...] = chosen_score[...]


def local(
    queries,
    new_keys,
    new_values,
    cache_keys,
    cache_values,
    lengths,
    out_weight,
    resid_expert,
    gain_expert,
    hidden_amateur,
    gain_amateur,
    head_expert,
    head_amateur,
    chosen,
):
    vmem = pl.BlockSpec(memory_space=pltpu.VMEM)
    hbm = pl.BlockSpec(memory_space=pl.ANY)
    dma = pltpu.SemaphoreType.DMA
    scores, chosen_score = pl.pallas_call(
        kernel,
        out_shape=(
            jax.ShapeDtypeStruct((64, 4, 512), BF16),
            jax.ShapeDtypeStruct((4, 64), F32),
        ),
        in_specs=[pl.BlockSpec(memory_space=pltpu.SMEM)] + [vmem] * 8 + [hbm] * 5,
        out_specs=(vmem, vmem),
        scratch_shapes=[
            pltpu.VMEM((4, 32, 1024), BF16),
            pltpu.VMEM((4, 32, 1024), BF16),
            pltpu.VMEM((512, 512), BF16),
            pltpu.VMEM((512, 8192), BF16),
            pltpu.VMEM((512, 4096), BF16),
            pltpu.VMEM((16, 80, 128), BF16),
            pltpu.VMEM((16, 80, 128), BF16),
            pltpu.VMEM((128, 128), F32),
            pltpu.VMEM((2, 8, 4, 16, 128), BF16),
            pltpu.VMEM((2, 8, 16, 512), BF16),
            pltpu.VMEM((16, 16, 512), BF16),
            pltpu.VMEM((2, 8, 4, 4, 16, 512), BF16),
            pltpu.VMEM((2, 8, 4, 80, 256), BF16),
            pltpu.VMEM((512, 256), F32),
            pltpu.VMEM((512, 256), F32),
            pltpu.VMEM((256, 128), F32),
            pltpu.VMEM((256, 128), F32),
            pltpu.VMEM((256, 512), F32),
            pltpu.VMEM((8, 128), F32),
            pltpu.VMEM((2, 8, 128), F32),
            pltpu.VMEM((16, 8, 128), F32),
            pltpu.VMEM((8, 8, 128), F32),
            pltpu.VMEM((2, 8, 128), F32),
            dma((5,)),
            dma((2,)),
            dma((4,)),
            dma((2,)),
            dma,
            dma((8,)),
            dma((2,)),
            dma((2,)),
            dma((8,)),
            dma((4, 8)),
            dma((8,)),
            dma((8,)),
            dma((3,)),
            dma((3,)),
            dma((4,)),
            dma((4,)),
        ],
        compiler_params=pltpu.CompilerParams(
            collective_id=0, has_side_effects=True, vmem_limit_bytes=56 * 1024 * 1024
        ),
        name="contrast",
    )(
        lengths,
        queries,
        new_keys,
        new_values,
        resid_expert,
        gain_expert,
        gain_amateur,
        hidden_amateur,
        chosen.T,
        cache_keys,
        cache_values,
        out_weight,
        head_expert,
        head_amateur,
    )
    scores, chosen_score = pl.pallas_call(
        finish,
        out_shape=(
            jax.ShapeDtypeStruct((64, 4, 512), BF16),
            jax.ShapeDtypeStruct((4, 64), F32),
        ),
        in_specs=[vmem] * 2,
        out_specs=(vmem, vmem),
        name="finish",
    )(scores, chosen_score)
    return scores, chosen_score.T


def solution(mesh):
    return jax.shard_map(
        local,
        mesh=mesh,
        in_specs=(
            P("dp", None, None),
            P("dp", None, None),
            P("dp", None, None),
            P("dp", "mp", None),
            P("dp", "mp", None),
            P("dp"),
            P("mp", ("section", "dp")),
            P(None, ("section", "dp")),
            P(("section", "dp")),
            P(None, ("section", "dp")),
            P(("section", "dp")),
            P(("section", "dp", "mp"), None),
            P(("section", "dp", "mp"), None),
            P(),
        ),
        out_specs=(P(None, None, ("section", "dp", "mp")), P()),
        check_vma=False,
    )
```

time: 92.2 us -> 82.5 us (0.89)
  local copies, waits for them, and re-layouts: 5.44 us -> 0 us
  Pallas kernels: 85.9 us -> 81.7 us
    pallas_call x1 -> x2, Pallas kernels: 85.9 us -> 81.7 us  [the longest x1 80 us: local(): pl.pallas_call(kernel, out_shape=(jax.ShapeDtypeStruct((64, 4, 512), BF16...]
    reshape x3 -> x0, local copies, waits for them, and re-layouts: 4.2 us -> none  [the longest x1 1.72 us: local(): return (scores.reshape(64, 4, 512), chosen_score.T)]
    unnamed x1 -> x0, local copies, waits for them, and re-layouts: 1.25 us -> none
where the time goes in v2:
time: 82.5 us; the launch traced here: 82.4 us
  Pallas kernels  81.7 us (99%)
    pallas_call x1, Pallas kernels, local(): pl.pallas_call(kernel, out_shape=(jax.ShapeDtypeStruct((64, 4, 512), BF16...  80 us
    pallas_call x1, Pallas kernels, local(): pl.pallas_call(finish, out_shape=(jax.ShapeDtypeStruct((64, 4, 512), BF16...  1.68 us

profile of v2, /device:TPU:1, one launch (start us, length us, event | category | flops | bytes accessed | tf_op | source)
XLA Modules:
  0.0 82.4 jit_solution(14997954184828025895)
XLA Ops:
  0.6 80.0 %contrast.1 = (bf16[64,4,512]{2,1,0:T(4,128)(2,1)}, f32[4,64]{1,0:T(4,128)}) custom-call(s32[8]{0:T(128)} %lengths.1, bf16[8,4,8192]{2,1,0:T(4,128)(2,1)} %queries.1, bf16[8,4,1024]{2,1,0:T(4,128)(2,1)} %new_keys.1, bf16[8,4,1024]{2,1,0:T(4,128)(2,1)} %new_values.1, bf16[256,512]{1,0:T(8,128)(2,1)} %resid.1, bf16[512]{0:T(512)(128)(2,1)} %gain_expert.1, ...), custom_call_target="tpu_custom_call" | custom-call | tf_op jit(solution)/shard_map/contrast/pallas_call | solution.py:588
  80.7 1.7 %finish.1 = (bf16[64,4,512]{2,1,0:T(4,128)(2,1)}, f32[4,64]{1,0:T(4,128)}) custom-call(bf16[64,4,512]{2,1,0:T(4,128)(2,1)} %get-tuple-element.6.scores, f32[4,64]{1,0:T(4,128)} %get-tuple-element.7.chosen_score), custom_call_target="tpu_custom_call" | custom-call | tf_op jit(solution)/shard_map/finish/pallas_call | solution.py:657

commit v3 on v2

--- a/solution.py
+++ b/solution.py
@@ -68,10 +68,8 @@
     square_a,
     diff,
     stats_s,
-    stats_h,
     stats_p,
     stats_z,
-    stats_f,
     load_sem,
     state_sem,
     attended_sem,
@@ -86,6 +84,8 @@
     relay_recv,
     am_send,
     am_recv,
+    am_rsend,
+    am_rrecv,
     stats_send,
     stats_recv,
 ):
@@ -129,19 +129,18 @@
         )
         return carry
 
-    def greet_z(k, carry):
+    def greet_n(k, carry):
         pl.semaphore_signal(
-            barrier, inc=1, device_id=at_z((z + k) % 8), device_id_type=MESH
-        )
-        return carry
-
-    lax.fori_loop(1, 8, greet_z, 0)
+            barrier, inc=1, device_id=at_n((n + k) % 16), device_id_type=MESH
+        )
+        return carry
+
+    lax.fori_loop(1, 16, greet_n, 0)
     lax.fori_loop(1, 16, greet_mp, 0)
-    pl.semaphore_signal(barrier, inc=1, device_id=sibling, device_id_type=MESH)
     for load in loads:
         load.start()
 
-    amateur[c, z, u, 0:64, :] = hidden_amateur[pl.ds(pl.multiple_of(u * 64, 64), 64), :]
+    amateur[c, z, 0:256, :] = hidden_amateur[...]
     row16 = iota((16, 256), 0)
     gains = jnp.where(
         row16 == 0,
@@ -152,7 +151,7 @@
             jnp.where(row16 == 2, gain_amateur[...].astype(F32).reshape(1, 256), 0.0),
         ),
     )
-    amateur[c, z, u, 64:80, :] = gains.astype(BF16)
+    amateur[c, z, 256:272, :] = gains.astype(BF16)
 
     row_i, col_i = iota((128, 128), 0), iota((128, 128), 1)
     limit = jnp.zeros((128, 128), jnp.int32)
@@ -206,7 +205,7 @@
         return carry
 
     lax.fori_loop(0, 8, attend, 0)
-    pl.semaphore_wait(barrier, 23)
+    pl.semaphore_wait(barrier, 30)
 
     def send_state(k, carry):
         dest = (mp + k) % 16
@@ -217,12 +216,31 @@
 
     lax.fori_loop(1, 16, send_state, 0)
 
-    def send_am(k, carry):
-        ref = amateur.at[c, z, u]
-        rcopy(ref, ref, am_send.at[0], am_recv.at[0], at_z((z + k) % 8)).start()
-        return carry
-
-    lax.fori_loop(1, 8, send_am, 0)
+    def am_copy(way, step):
+        if way == 0:
+            shard, target = (z - step + 9) % 8, (z + 1) % 8
+        else:
+            shard, target = (z + step - 1) % 8, (z + 7) % 8
+        ref = amateur.at[c, shard]
+        return rcopy(ref, ref, am_send.at[way, step], am_recv.at[way, step], at_z(target))
+
+    def am_relay(shard, cc):
+        ref = amateur.at[cc, shard]
+        return rcopy(ref, ref, am_rsend.at[shard], am_rrecv.at[shard], sibling)
+
+    def am_advance(step):
+        am_copy(0, step).wait_recv()
+        if step < 4:
+            am_copy(1, step).wait_recv()
+            am_copy(0, step + 1).start()
+            if step < 3:
+                am_copy(1, step + 1).start()
+            am_relay((z + step) % 8, c).start()
+        am_relay((z - step + 8) % 8, c).start()
+
+    am_copy(0, 1).start()
+    am_copy(1, 1).start()
+    am_relay(z, c).start()
     state_in[mp] = state_out[mp]
     fifteen = pl.ds(0, 15)
     state_all = rcopy(
@@ -246,73 +264,38 @@
     for k in range(16):
         mixed = mixed + own[:, k : k + 1] * state_in[k, 0:64, :].astype(F32)
 
-    attended[c, z] = mixed.astype(BF16).reshape(4, 16, HD)
+    block = dp * 2 + sec
+    attended[block] = mixed.astype(BF16).reshape(4, 16, HD)
 
     def send_attended(k, carry):
-        ref = attended.at[c, z]
-        rcopy(ref, ref, attended_sem.at[0], attended_sem.at[1], at_z((z + k) % 8)).start()
-        return carry
-
-    lax.fori_loop(1, 8, send_attended, 0)
-
-    am_one = amateur.at[c, pl.ds(0, 7), u]
-    am_first = rcopy(am_one, am_one, am_send.at[0], am_recv.at[0], sibling)
-    am_first.wait_recv()
-
-    def send_quarter(k, carry):
-        ref = amateur.at[c, :, u, pl.ds(0, 64)]
-        rcopy(ref, ref, am_send.at[1], am_recv.at[1], at_uv((u + k) % 4, v)).start()
-        return carry
-
-    lax.fori_loop(1, 4, send_quarter, 0)
+        ref = attended.at[block]
+        rcopy(ref, ref, attended_sem.at[0], attended_sem.at[1], at_n((n + k) % 16)).start()
+        return carry
+
+    lax.fori_loop(1, 16, send_attended, 0)
     loads[2].wait()
-    seven = attended.at[c, pl.ds(0, 7)]
-    attended_all = rcopy(seven, seven, attended_sem.at[0], attended_sem.at[1], sibling)
+    fifteen_a = attended.at[fifteen]
+    attended_all = rcopy(fifteen_a, fifteen_a, attended_sem.at[0], attended_sem.at[1], sibling)
     attended_all.wait_recv()
-
-    def pass_attended(cc):
-        ref = attended.at[cc]
-        return rcopy(ref, ref, attended_sem.at[2], attended_sem.at[3], sibling)
-
-    pass_attended(c).start()
-
-    def project(cc):
-        partial = jnp.zeros((128, 512), F32)
-        for h in range(4):
-            partial = partial + jnp.dot(
-                attended[cc, :, h].reshape(128, HD),
-                weight_v[h * HD : (h + 1) * HD, :],
-                preferred_element_type=F32,
-            )
-        part_out[cc] = partial.astype(BF16).reshape(8, 16, 512)
-
-        def send_part(zz, carry):
-            dest = (zz % 4) * 4 + cc * 2 + zz // 4
-
-            @pl.when(dest != mp)
-            def _():
-                rcopy(
-                    part_out.at[cc, zz], part_in.at[mp], part_sem.at[0], part_sem.at[1], at_mp(dest)
-                ).start()
-
-            return carry
-
-        lax.fori_loop(0, 8, send_part, 0)
-
-    project(c)
-    pass_attended(1 - c).wait_recv()
-    project(1 - c)
-    part_in[mp] = part_out[(mp // 2) % 2, (mp % 2) * 4 + mp // 4]
-
-    am_two = amateur.at[c, :, pl.ds(0, 3), pl.ds(0, 64)]
-    am_second = rcopy(am_two, am_two, am_send.at[1], am_recv.at[1], sibling)
-    am_second.wait_recv()
-
-    def am_pass(cc):
-        ref = amateur.at[cc]
-        return rcopy(ref, ref, am_send.at[2], am_recv.at[2], sibling)
-
-    am_pass(c).start()
+    partial = jnp.zeros((256, 512), F32)
+    for h in range(4):
+        partial = partial + jnp.dot(
+            attended[:, h].reshape(256, HD),
+            weight_v[h * HD : (h + 1) * HD, :],
+            preferred_element_type=F32,
+        )
+    part_out[...] = partial.astype(BF16).reshape(16, 16, 512)
+
+    def send_part(k, carry):
+        dest = (mp + k) % 16
+        rcopy(
+            part_out.at[dest], part_in.at[mp], part_sem.at[0], part_sem.at[1], at_mp(dest)
+        ).start()
+        return carry
+
+    lax.fori_loop(1, 16, send_part, 0)
+    part_in[mp] = part_out[mp]
+    am_advance(1)
     part_all = rcopy(
         part_in.at[fifteen], part_in.at[fifteen], part_sem.at[0], part_sem.at[1], sibling
     )
@@ -321,14 +304,15 @@
     projected = part_in[0].astype(F32)
     for k in range(1, 16):
         projected = projected + part_in[k].astype(F32)
-    full[c, z, v, u] = (hidden + projected).astype(BF16)
-
-    def one(block, target):
-        ref = full.at[c, block, v, u]
-        return rcopy(ref, ref, one_send, one_recv.at[block], at_z(target))
+    full[c, 3, v, u] = (hidden + projected).astype(BF16)
+
+    def one(slot, target):
+        return rcopy(
+            full.at[c, 3, v, u], full.at[c, slot, v, u], one_send, one_recv.at[slot], at_z(target)
+        )
 
     def send_one(k, carry):
-        one(z, (z + k) % 8).start()
+        one((11 - k) % 8, (z + k) % 8).start()
         return carry
 
     lax.fori_loop(1, 8, send_one, 0)
@@ -352,7 +336,7 @@
     for half in range(2):
 
         def wait_one(zz, carry):
-            @pl.when(zz != z)
+            @pl.when(zz != 3)
             def _():
                 one(zz, z).wait_recv()
 
@@ -362,33 +346,35 @@
         for k in range(1, 4):
             two(half, k).start()
 
+    am_advance(2)
+
     def two_all(half):
         ref = full.at[c, pl.ds(half * 4, 4), v, pl.ds(0, 3)]
         return rcopy(ref, ref, two_send.at[half], two_recv.at[half], sibling)
 
-    for half in range(2):
-        two_all(half).wait_recv()
-
-        def send_three(zz, carry):
-            for k in (2, 1, 3):
-                three(k, zz, v).start()
-            return carry
-
-        lax.fori_loop(half * 4, half * 4 + 4, send_three, 0)
+    def send_three(zz, carry):
+        for k in (2, 1, 3):
+            three(k, zz, v).start()
+        return carry
+
+    two_all(0).wait_recv()
+    lax.fori_loop(0, 4, send_three, 0)
+    am_advance(3)
 
     loads[3].wait()
     acc_a[...] = jnp.zeros_like(acc_a)
     acc_e[...] = jnp.zeros_like(acc_e)
     square_a[...] = jnp.zeros_like(square_a)
     square_e[...] = jnp.zeros_like(square_e)
-    am_pass(1 - c).wait_recv()
-
-    def am_block(k, carry):
+
+    def am_block(j, carry):
+        k = (z + 5 + j) % 8
+        am_relay(k, 1 - c).wait_recv()
         parts = []
         squares = square_a[...]
         for cc in range(2):
-            wide = amateur[cc, k, :, 0:64, :].reshape(256, 256).astype(F32)
-            gain = amateur[cc, k, x if cc == 0 else y, 64:80, :].astype(F32)[2:3]
+            wide = amateur[cc, k, 0:256, :].astype(F32)
+            gain = amateur[cc, k, 256:272, :].astype(F32)[2:3]
             squares = squares + wide[:, 0:128] * wide[:, 0:128] + wide[:, 128:] * wide[:, 128:]
             parts.append((wide * gain).astype(BF16))
         square_a[...] = squares
@@ -400,7 +386,7 @@
         )
         return carry
 
-    lax.fori_loop(0, 8, am_block, 0)
+    lax.fori_loop(0, 7, am_block, 0)
     ones = jnp.ones((8, 128), F32)
 
     def inverse_norm(ref, width):
@@ -409,11 +395,87 @@
         )
         return lax.rsqrt(sums[0:1] / width + EPSILON)
 
-    logits_a = acc_a[...] * inverse_norm(square_a, 4096.0)
-    acc_a[...] = logits_a
-    top_a = jnp.max(logits_a, axis=0, keepdims=True)
-    total_a = jnp.sum(jnp.exp(logits_a - top_a), axis=0, keepdims=True)
-
+    row8 = iota((8, 128), 0)
+
+    def pack(rows):
+        tile = jnp.zeros((8, 128), F32)
+        for k, row in enumerate(rows):
+            tile = jnp.where(row8 == k, row, tile)
+        return tile
+
+    def halves(rows):
+        return pack([row[:, h * 128 : h * 128 + 128] for row in rows for h in range(2)])
+
+    def join(tiles):
+        top = tiles[0]
+        for tile in tiles[1:]:
+            top = jnp.maximum(top, tile)
+        top = top[0:2]
+        total, pick = jnp.zeros((2, 128), F32), jnp.zeros((2, 128), F32)
+        for tile in tiles:
+            total = total + tile[2:4] * jnp.exp(tile[0:2] - top)
+            pick = pick + tile[4:6]
+        return top, total, pick
+
+    def joined(tiles):
+        return pack([part[h : h + 1] for part in join(tiles) for h in range(2)])
+
+    fifteen_p = stats_p.at[0, fifteen]
+    seven_z = stats_z.at[0, pl.ds(0, 7)]
+
+    def pair(which):
+        return rcopy(
+            stats_s.at[which, 0],
+            stats_s.at[which, 1],
+            stats_send.at[which, 0],
+            stats_recv.at[which, 0],
+            sibling,
+        )
+
+    def start_pair(which, rows):
+        stats_s[which, 0] = halves(rows)
+        pair(which).start()
+
+    def start_p(which):
+        pair(which).wait_recv()
+        stats_p[which, mp] = joined([stats_s[which, 0], stats_s[which, 1]])
+
+        def send_p(k, carry):
+            ref = stats_p.at[which, mp]
+            rcopy(
+                ref, ref, stats_send.at[which, 1], stats_recv.at[which, 1], at_mp((mp + k) % 16)
+            ).start()
+            return carry
+
+        lax.fori_loop(1, 16, send_p, 0)
+
+    def p_all(which):
+        return rcopy(
+            fifteen_p, fifteen_p, stats_send.at[which, 1], stats_recv.at[which, 1], sibling
+        )
+
+    def start_z(which):
+        p_all(which).wait_recv()
+        stats_z[which, z] = joined([stats_p[which, k] for k in range(16)])
+
+        def send_z(k, carry):
+            ref = stats_z.at[which, z]
+            rcopy(
+                ref, ref, stats_send.at[which, 2], stats_recv.at[which, 2], at_z((z + k) % 8)
+            ).start()
+            return carry
+
+        lax.fori_loop(1, 8, send_z, 0)
+
+    def z_all(which):
+        return rcopy(seven_z, seven_z, stats_send.at[which, 2], stats_recv.at[which, 2], sibling)
+
+    def settle(which):
+        pair(which).wait_send()
+        p_all(which).wait_send()
+        z_all(which).wait_send()
+
+    two_all(1).wait_recv()
     loads[4].wait()
 
     def gather_block(zz, carry):
@@ -422,6 +484,11 @@
             for k in (1, 3, 2):
                 three(k, zz, (v - k + 4) % 4).wait_recv()
             relay(zz, c).start()
+
+            @pl.when(zz < 4)
+            def _():
+                send_three(zz + 4, 0)
+
 
         @pl.when(zz >= 1)
         def _():
@@ -434,7 +501,7 @@
                 if cc == 0:
                     wide = jnp.swapaxes(wide, 0, 1)
                 wide = wide.reshape(256, 512).astype(F32)
-                tile = amateur[cc, k, x if cc == 0 else y, 64:80, :].astype(F32)
+                tile = amateur[cc, (z + 5 + k) % 8, 256:272, :].astype(F32)
                 for half in range(2):
                     piece = wide[:, half * 256 : half * 256 + 256]
                     squares = (
@@ -445,7 +512,7 @@
                     parts.append((piece * tile[half : half + 1]).astype(BF16))
             square_e[...] = squares
             acc_e[...] += lax.dot_general(
-                he_v[:, pl.ds(pl.multiple_of(k * 1024, 1024), 1024)],
+                he_v[:, pl.ds(pl.multiple_of((z + 5 + k) % 8 * 1024, 1024), 1024)],
                 jnp.concatenate(parts, axis=1),
                 NT,
                 preferred_element_type=F32,
@@ -453,7 +520,18 @@
 
         return carry
 
-    lax.fori_loop(0, 9, gather_block, 0)
+    lax.fori_loop(0, 3, gather_block, 0)
+    am_advance(4)
+    lax.fori_loop(3, 4, gather_block, 0)
+    lax.fori_loop(7, 8, am_block, 0)
+    logits_a = acc_a[...] * inverse_norm(square_a, 4096.0)
+    acc_a[...] = logits_a
+    top_a = jnp.max(logits_a, axis=0, keepdims=True)
+    total_a = jnp.sum(jnp.exp(logits_a - top_a), axis=0, keepdims=True)
+    start_pair(1, (top_a, total_a))
+    lax.fori_loop(4, 6, gather_block, 0)
+    start_p(1)
+    lax.fori_loop(6, 9, gather_block, 0)
 
     logits_e = acc_e[...] * inverse_norm(square_e, 8192.0)
     top_e = jnp.max(logits_e, axis=0, keepdims=True)
@@ -472,49 +550,17 @@
     matched = iota((512, 256), 0).astype(F32) == target
     picked = jnp.sum(jnp.where(matched, difference, 0.0), axis=0, keepdims=True)
 
-    row8 = iota((8, 128), 0)
-
-    def pack(rows, half):
-        tile = jnp.zeros((8, 128), F32)
-        for k, row in enumerate(rows):
-            tile = jnp.where(row8 == k, row[:, half * 128 : half * 128 + 128], tile)
-        return tile
-
-    def join(tiles):
-        top = tiles[0]
-        for tile in tiles[1:]:
-            top = jnp.maximum(top, tile)
-        te, ta = top[0:1], top[2:3]
-        zero = jnp.zeros((1, 128), F32)
-        se, sa, pick = zero, zero, zero
-        for tile in tiles:
-            se = se + tile[1:2] * jnp.exp(tile[0:1] - te)
-            sa = sa + tile[3:4] * jnp.exp(tile[2:3] - ta)
-            pick = pick + tile[4:5]
-        return te, se, ta, sa, pick
-
-    mine = (top_e, total_e, top_a, total_a, picked)
-    stats_h[0] = pack(mine, 0)
-    stats_h[1] = pack(mine, 1)
-    pair = rcopy(stats_h.at[1 - c], stats_s, stats_send.at[0], stats_recv.at[0], sibling)
-    pair.start()
-    pair.wait_recv()
-    stats_p[mp] = pack(join([stats_h[c], stats_s[...]]), 0)
-
-    def send_p(k, carry):
-        ref = stats_p.at[mp]
-        rcopy(ref, ref, stats_send.at[1], stats_recv.at[1], at_mp((mp + k) % 16)).start()
-        return carry
-
-    lax.fori_loop(1, 16, send_p, 0)
+    start_pair(0, (top_e, total_e, picked))
+    start_p(0)
+    start_z(1)
     diff[...] = difference.T
 
     state_all.wait_send()
     attended_all.wait_send()
-    pass_attended(c).wait_send()
-    am_first.wait_send()
-    am_second.wait_send()
-    am_pass(c).wait_send()
+    for step in range(1, 5):
+        am_copy(0, step).wait_send()
+        if step < 4:
+            am_copy(1, step).wait_send()
     part_all.wait_send()
     ref = full.at[c, pl.ds(0, 7), v, u]
     rcopy(ref, ref, one_send, one_recv.at[0], sibling).wait_send()
@@ -523,42 +569,30 @@
 
     def drain(k, carry):
         relay(k, c).wait_send()
+        am_relay(k, c).wait_send()
         ref = full.at[c, k, pl.ds(0, 3)]
         rcopy(ref, ref, three_send.at[k], three_recv.at[1, k], sibling).wait_send()
         return carry
 
     lax.fori_loop(0, 8, drain, 0)
-    pair.wait_send()
-    ref = stats_p.at[fifteen]
-    p_all = rcopy(ref, ref, stats_send.at[1], stats_recv.at[1], sibling)
-    p_all.wait_recv()
-    stats_z[z] = pack(join([stats_p[k] for k in range(16)]), 0)
-
-    def send_z(k, carry):
-        ref = stats_z.at[z]
-        rcopy(ref, ref, stats_send.at[2], stats_recv.at[2], at_z((z + k) % 8)).start()
-        return carry
-
-    lax.fori_loop(1, 8, send_z, 0)
-    p_all.wait_send()
-    ref = stats_z.at[pl.ds(0, 7)]
-    z_all = rcopy(ref, ref, stats_send.at[2], stats_recv.at[2], sibling)
-    z_all.wait_recv()
-    te, se, ta, sa, pick = join([stats_z[k] for k in range(8)])
-    shift = te + jnp.log(se) - CONTRAST * (ta + jnp.log(sa))
-    stats_f[c] = pack((shift, pick - shift), 0)
-    last = rcopy(stats_f.at[c], stats_f.at[c], stats_send.at[3], stats_recv.at[3], sibling)
-    last.start()
-    z_all.wait_send()
-    last.wait_recv()
-    both = jnp.concatenate([stats_f[0], stats_f[1]], axis=1)
-    shift_t = jnp.concatenate([both] * 16, axis=0).T
+    start_z(0)
+    settle(1)
+    z_all(1).wait_recv()
+    top, total, _ = join([stats_z[1, k] for k in range(8)])
+    lse_a = top + jnp.log(total)
+    z_all(0).wait_recv()
+    top, total, pick = join([stats_z[0, k] for k in range(8)])
+    shift = top + jnp.log(total) - CONTRAST * lse_a
+    chosen_row = pick - shift
+    shift = jnp.concatenate([shift[0:1], shift[1:2]], axis=1)
+    chosen_row = jnp.concatenate([chosen_row[0:1], chosen_row[1:2]], axis=1)
+    shift_t = jnp.broadcast_to(shift, (128, 256)).T
     out[...] = (diff[...] - shift_t[:, 0:1]).reshape(64, 4, 512).astype(BF16)
-    masked = jnp.where(step_row, both[1:2], 0.0)
+    masked = jnp.where(step_row, chosen_row, 0.0)
     out_chosen[...] = lax.dot_general(
         masked, pick_row, NT, preferred_element_type=F32, precision=lax.Precision.HIGHEST
     )[0:4]
-    last.wait_send()
+    settle(0)
 
 
 def finish(scores, chosen_score, out, out_chosen):
@@ -602,24 +636,22 @@
             pltpu.VMEM((16, 80, 128), BF16),
             pltpu.VMEM((16, 80, 128), BF16),
             pltpu.VMEM((128, 128), F32),
-            pltpu.VMEM((2, 8, 4, 16, 128), BF16),
-            pltpu.VMEM((2, 8, 16, 512), BF16),
+            pltpu.VMEM((16, 4, 16, 128), BF16),
+            pltpu.VMEM((16, 16, 512), BF16),
             pltpu.VMEM((16, 16, 512), BF16),
             pltpu.VMEM((2, 8, 4, 4, 16, 512), BF16),
-            pltpu.VMEM((2, 8, 4, 80, 256), BF16),
+            pltpu.VMEM((2, 8, 272, 256), BF16),
             pltpu.VMEM((512, 256), F32),
             pltpu.VMEM((512, 256), F32),
             pltpu.VMEM((256, 128), F32),
             pltpu.VMEM((256, 128), F32),
             pltpu.VMEM((256, 512), F32),
-            pltpu.VMEM((8, 128), F32),
-            pltpu.VMEM((2, 8, 128), F32),
-            pltpu.VMEM((16, 8, 128), F32),
-            pltpu.VMEM((8, 8, 128), F32),
-            pltpu.VMEM((2, 8, 128), F32),
+            pltpu.VMEM((2, 2, 8, 128), F32),
+            pltpu.VMEM((2, 16, 8, 128), F32),
+            pltpu.VMEM((2, 8, 8, 128), F32),
             dma((5,)),
             dma((2,)),
-            dma((4,)),
+            dma((2,)),
             dma((2,)),
             dma,
             dma((8,)),
@@ -629,10 +661,12 @@
             dma((4, 8)),
             dma((8,)),
             dma((8,)),
-            dma((3,)),
-            dma((3,)),
-            dma((4,)),
-            dma((4,)),
+            dma((2, 5)),
+            dma((2, 5)),
+            dma((8,)),
+            dma((8,)),
+            dma((2, 3)),
+            dma((2, 3)),
         ],
         compiler_params=pltpu.CompilerParams(
             collective_id=0, has_side_effects=True, vmem_limit_bytes=56 * 1024 * 1024

time: 82.5 us -> 76.8 us (0.931)
  Pallas kernels: 81.7 us -> 75.3 us
    pallas_call x1, Pallas kernels: 80 us -> 73.6 us  [local(): pl.pallas_call(kernel, out_shape=(jax.ShapeDtypeStruct((64, 4, 512), BF16...]
where the time goes in v3:
time: 76.8 us; the launch traced here: 75.9 us
  Pallas kernels  75.3 us (98%)
    pallas_call x1, Pallas kernels, local(): pl.pallas_call(kernel, out_shape=(jax.ShapeDtypeStruct((64, 4, 512), BF16...  73.6 us
    pallas_call x1, Pallas kernels, local(): pl.pallas_call(finish, out_shape=(jax.ShapeDtypeStruct((64, 4, 512), BF16...  1.68 us

profile of v3, /device:TPU:1, one launch (start us, length us, event | category | flops | bytes accessed | tf_op | source)
XLA Modules:
  0.0 75.9 jit_solution(16837257831077976881)
XLA Ops:
  0.6 73.6 %contrast.1 = (bf16[64,4,512]{2,1,0:T(4,128)(2,1)}, f32[4,64]{1,0:T(4,128)}) custom-call(s32[8]{0:T(128)} %lengths.1, bf16[8,4,8192]{2,1,0:T(4,128)(2,1)} %queries.1, bf16[8,4,1024]{2,1,0:T(4,128)(2,1)} %new_keys.1, bf16[8,4,1024]{2,1,0:T(4,128)(2,1)} %new_values.1, bf16[256,512]{1,0:T(8,128)(2,1)} %resid.1, bf16[512]{0:T(512)(128)(2,1)} %gain_expert.1, ...), custom_call_target="tpu_custom_call" | custom-call | tf_op jit(solution)/shard_map/contrast/pallas_call | solution.py:622
  74.3 1.7 %finish.1 = (bf16[64,4,512]{2,1,0:T(4,128)(2,1)}, f32[4,64]{1,0:T(4,128)}) custom-call(bf16[64,4,512]{2,1,0:T(4,128)(2,1)} %get-tuple-element.6.scores, f32[4,64]{1,0:T(4,128)} %get-tuple-element.7.chosen_score), custom_call_target="tpu_custom_call" | custom-call | tf_op jit(solution)/shard_map/finish/pallas_call | solution.py:691

commit v4 on v3

--- a/solution.py
+++ b/solution.py
@@ -30,6 +30,14 @@
 
 def iota(shape, dim):
     return lax.broadcasted_iota(jnp.int32, shape, dim)
+
+
+def place(i):
+    return (2 - i + 3 * (i // 2) + 2 * (i // 3)) % 4
+
+
+def hop(k):
+    return (4 + (k + 1) // 2 * (1 - 2 * (k % 2))) % 8
 
 
 def kernel(
@@ -49,6 +57,10 @@
     head_amateur,
     out,
     out_chosen,
+    queries_v,
+    new_keys_v,
+    new_values_v,
+    resid_v,
     keys_v,
     values_v,
     weight_v,
@@ -111,36 +123,51 @@
     def at_uv(uu, vv):
         return (sec, dp, (uu * 4 + vv) * (1 - c) + (vv * 4 + uu) * c)
 
+    def far_mp(k):
+        return (x + place(k % 4)) % 4 * 4 + (y + place(k // 4)) % 4
+
+    def far_n(k):
+        return (z + hop(k // 2)) % 8 * 2 + (c + 1 + k) % 2
+
     sibling = (sec, dp + 1 - 2 * c, mp)
 
+    mine = pl.ds(sec * 4, 4)
     loads = [
         pltpu.make_async_copy(cache_keys.at[pl.ds(sec * 4, 4)], keys_v, load_sem.at[0]),
         pltpu.make_async_copy(cache_values.at[pl.ds(sec * 4, 4)], values_v, load_sem.at[1]),
         pltpu.make_async_copy(out_weight, weight_v, load_sem.at[2]),
         pltpu.make_async_copy(head_amateur, ha_v, load_sem.at[3]),
         pltpu.make_async_copy(head_expert, he_v, load_sem.at[4]),
+        pltpu.make_async_copy(
+            resid.at[pl.ds(pl.multiple_of(mp * 16, 16), 16)], resid_v, load_sem.at[5]
+        ),
+    ]
+    first_loads = [
+        pltpu.make_async_copy(queries.at[mine], queries_v, load_sem.at[6]),
+        pltpu.make_async_copy(new_keys.at[mine], new_keys_v, load_sem.at[7]),
+        pltpu.make_async_copy(new_values.at[mine], new_values_v, load_sem.at[8]),
+        pltpu.make_async_copy(hidden_amateur, amateur.at[c, z, pl.ds(0, 256)], load_sem.at[9]),
     ]
 
     barrier = pltpu.get_barrier_semaphore()
 
     def greet_mp(k, carry):
         pl.semaphore_signal(
-            barrier, inc=1, device_id=at_mp((mp + k) % 16), device_id_type=MESH
+            barrier, inc=1, device_id=at_mp(far_mp(k)), device_id_type=MESH
         )
         return carry
 
     def greet_n(k, carry):
         pl.semaphore_signal(
-            barrier, inc=1, device_id=at_n((n + k) % 16), device_id_type=MESH
-        )
-        return carry
-
-    lax.fori_loop(1, 16, greet_n, 0)
-    lax.fori_loop(1, 16, greet_mp, 0)
-    for load in loads:
+            barrier, inc=1, device_id=at_n(far_n(k)), device_id_type=MESH
+        )
+        return carry
+
+    lax.fori_loop(0, 15, greet_n, 0)
+    lax.fori_loop(0, 15, greet_mp, 0)
+    for load in first_loads + loads:
         load.start()
 
-    amateur[c, z, 0:256, :] = hidden_amateur[...]
     row16 = iota((16, 256), 0)
     gains = jnp.where(
         row16 == 0,
@@ -160,11 +187,11 @@
     live_old = (row_i // 32 == (col_i // 4) % 4) & (row_i % 32 + mp * 32 < limit)
     row_n, col_n = iota((16, 128), 0), iota((16, 128), 1)
     live_new = (row_n // 4 == (col_n // 4) % 4) & (row_n % 4 <= col_n % 4) & (mp == 0)
-    loads[0].wait()
-    loads[1].wait()
+    for load in first_loads + loads[0:2]:
+        load.wait()
 
     def stacked(ref, start):
-        part = ref[pl.ds(sec * 4, 4), :, pl.ds(start, HD)].astype(F32)
+        part = ref[:, :, pl.ds(start, HD)].astype(F32)
         return jnp.concatenate([part[r] for r in range(4)], axis=0)
 
     def attend(i, carry):
@@ -172,10 +199,10 @@
         base = pl.multiple_of(g * HD, HD)
         keys_old = keys_v[:, :, pl.ds(base, HD)].reshape(128, HD)
         values_old = values_v[:, :, pl.ds(base, HD)].reshape(128, HD)
-        keys_new = stacked(new_keys, base).astype(BF16)
-        values_new = stacked(new_values, base).astype(BF16)
+        keys_new = stacked(new_keys_v, base).astype(BF16)
+        values_new = stacked(new_values_v, base).astype(BF16)
         query = jnp.concatenate(
-            [stacked(queries, pl.multiple_of(g * 1024 + h * HD, HD)) for h in range(8)], axis=0
+            [stacked(queries_v, pl.multiple_of(g * 1024 + h * HD, HD)) for h in range(8)], axis=0
         ).astype(BF16)
         scaling = 1.0 / HD**0.5
         s_old = lax.dot_general(keys_old, query, NT, preferred_element_type=F32) * scaling
@@ -208,13 +235,13 @@
     pl.semaphore_wait(barrier, 30)
 
     def send_state(k, carry):
-        dest = (mp + k) % 16
+        dest = far_mp(k)
         rcopy(
             state_out.at[dest], state_in.at[mp], state_sem.at[0], state_sem.at[1], at_mp(dest)
         ).start()
         return carry
 
-    lax.fori_loop(1, 16, send_state, 0)
+    lax.fori_loop(0, 15, send_state, 0)
 
     def am_copy(way, step):
         if way == 0:
@@ -269,11 +296,12 @@
 
     def send_attended(k, carry):
         ref = attended.at[block]
-        rcopy(ref, ref, attended_sem.at[0], attended_sem.at[1], at_n((n + k) % 16)).start()
-        return carry
-
-    lax.fori_loop(1, 16, send_attended, 0)
+        rcopy(ref, ref, attended_sem.at[0], attended_sem.at[1], at_n(far_n(k))).start()
+        return carry
+
+    lax.fori_loop(0, 15, send_attended, 0)
     loads[2].wait()
+    loads[5].wait()
     fifteen_a = attended.at[fifteen]
     attended_all = rcopy(fifteen_a, fifteen_a, attended_sem.at[0], attended_sem.at[1], sibling)
     attended_all.wait_recv()
@@ -287,20 +315,20 @@
     part_out[...] = partial.astype(BF16).reshape(16, 16, 512)
 
     def send_part(k, carry):
-        dest = (mp + k) % 16
+        dest = far_mp(k)
         rcopy(
             part_out.at[dest], part_in.at[mp], part_sem.at[0], part_sem.at[1], at_mp(dest)
         ).start()
         return carry
 
-    lax.fori_loop(1, 16, send_part, 0)
+    lax.fori_loop(0, 15, send_part, 0)
     part_in[mp] = part_out[mp]
     am_advance(1)
     part_all = rcopy(
         part_in.at[fifteen], part_in.at[fifteen], part_sem.at[0], part_sem.at[1], sibling
     )
     part_all.wait_recv()
-    hidden = resid[pl.ds(pl.multiple_of(mp * 16, 16), 16), :].astype(F32)
+    hidden = resid_v[...].astype(F32)
     projected = part_in[0].astype(F32)
     for k in range(1, 16):
         projected = projected + part_in[k].astype(F32)
@@ -312,10 +340,10 @@
         )
 
     def send_one(k, carry):
-        one((11 - k) % 8, (z + k) % 8).start()
-        return carry
-
-    lax.fori_loop(1, 8, send_one, 0)
+        one((11 - hop(k)) % 8, (z + hop(k)) % 8).start()
+        return carry
+
+    lax.fori_loop(0, 7, send_one, 0)
 
     def two(half, k):
         ref = full.at[c, pl.ds(half * 4, 4), v, u]
@@ -443,11 +471,11 @@
         def send_p(k, carry):
             ref = stats_p.at[which, mp]
             rcopy(
-                ref, ref, stats_send.at[which, 1], stats_recv.at[which, 1], at_mp((mp + k) % 16)
+                ref, ref, stats_send.at[which, 1], stats_recv.at[which, 1], at_mp(far_mp(k))
             ).start()
             return carry
 
-        lax.fori_loop(1, 16, send_p, 0)
+        lax.fori_loop(0, 15, send_p, 0)
 
     def p_all(which):
         return rcopy(
@@ -461,11 +489,11 @@
         def send_z(k, carry):
             ref = stats_z.at[which, z]
             rcopy(
-                ref, ref, stats_send.at[which, 2], stats_recv.at[which, 2], at_z((z + k) % 8)
+                ref, ref, stats_send.at[which, 2], stats_recv.at[which, 2], at_z((z + hop(k)) % 8)
             ).start()
             return carry
 
-        lax.fori_loop(1, 8, send_z, 0)
+        lax.fori_loop(0, 7, send_z, 0)
 
     def z_all(which):
         return rcopy(seven_z, seven_z, stats_send.at[which, 2], stats_recv.at[which, 2], sibling)
@@ -625,9 +653,18 @@
             jax.ShapeDtypeStruct((64, 4, 512), BF16),
             jax.ShapeDtypeStruct((4, 64), F32),
         ),
-        in_specs=[pl.BlockSpec(memory_space=pltpu.SMEM)] + [vmem] * 8 + [hbm] * 5,
+        in_specs=[pl.BlockSpec(memory_space=pltpu.SMEM)]
+        + [hbm] * 4
+        + [vmem] * 2
+        + [hbm]
+        + [vmem]
+        + [hbm] * 5,
         out_specs=(vmem, vmem),
         scratch_shapes=[
+            pltpu.VMEM((4, 4, 8192), BF16),
+            pltpu.VMEM((4, 4, 1024), BF16),
+            pltpu.VMEM((4, 4, 1024), BF16),
+            pltpu.VMEM((16, 512), BF16),
             pltpu.VMEM((4, 32, 1024), BF16),
             pltpu.VMEM((4, 32, 1024), BF16),
             pltpu.VMEM((512, 512), BF16),
@@ -649,7 +686,7 @@
             pltpu.VMEM((2, 2, 8, 128), F32),
             pltpu.VMEM((2, 16, 8, 128), F32),
             pltpu.VMEM((2, 8, 8, 128), F32),
-            dma((5,)),
+            dma((10,)),
             dma((2,)),
             dma((2,)),
             dma((2,)),

time: 76.8 us -> 75.5 us (0.983)
  Pallas kernels: 75.3 us -> 74.3 us
    pallas_call x1, Pallas kernels: 73.6 us -> 72.6 us  [local(): pl.pallas_call(kernel, out_shape=(jax.ShapeDtypeStruct((64, 4, 512), BF16...]
where the time goes in v4:
time: 75.5 us; the launch traced here: 75 us
  Pallas kernels  74.3 us (98%)
    pallas_call x1, Pallas kernels, local(): pl.pallas_call(kernel, out_shape=(jax.ShapeDtypeStruct((64, 4, 512), BF16...  72.6 us
    pallas_call x1, Pallas kernels, local(): pl.pallas_call(finish, out_shape=(jax.ShapeDtypeStruct((64, 4, 512), BF16...  1.68 us

profile of v4, /device:TPU:1, one launch (start us, length us, event | category | flops | bytes accessed | tf_op | source)
XLA Modules:
  0.0 75.0 jit_solution(10208369696810306094)
XLA Ops:
  0.6 72.6 %contrast.1 = (bf16[64,4,512]{2,1,0:T(4,128)(2,1)}, f32[4,64]{1,0:T(4,128)}) custom-call(s32[8]{0:T(128)} %lengths.1, bf16[8,4,8192]{2,1,0:T(4,128)(2,1)} %queries.1, bf16[8,4,1024]{2,1,0:T(4,128)(2,1)} %new_keys.1, bf16[8,4,1024]{2,1,0:T(4,128)(2,1)} %new_values.1, bf16[256,512]{1,0:T(8,128)(2,1)} %resid.1, bf16[512]{0:T(512)(128)(2,1)} %gain_expert.1, ...), custom_call_target="tpu_custom_call" | custom-call | tf_op jit(solution)/shard_map/contrast/pallas_call | solution.py:650
  73.3 1.7 %finish.1 = (bf16[64,4,512]{2,1,0:T(4,128)(2,1)}, f32[4,64]{1,0:T(4,128)}) custom-call(bf16[64,4,512]{2,1,0:T(4,128)(2,1)} %get-tuple-element.6.scores, f32[4,64]{1,0:T(4,128)} %get-tuple-element.7.chosen_score), custom_call_target="tpu_custom_call" | custom-call | tf_op jit(solution)/shard_map/finish/pallas_call | solution.py:728

commit v5 on v4

--- a/solution.py
+++ b/solution.py
@@ -55,8 +55,8 @@
     out_weight,
     head_expert,
     head_amateur,
-    out,
-    out_chosen,
+    out_diff,
+    out_rows,
     queries_v,
     new_keys_v,
     new_values_v,
@@ -79,6 +79,7 @@
     square_e,
     square_a,
     diff,
+    target_v,
     stats_s,
     stats_p,
     stats_z,
@@ -180,6 +181,18 @@
     )
     amateur[c, z, 256:272, :] = gains.astype(BF16)
 
+    pick_row = (iota((64, 256), 1) // 4 == iota((64, 256), 0)).astype(F32)
+    step_row = iota((8, 256), 1) % 4 == iota((8, 256), 0)
+    spread = jnp.dot(
+        chosen[...].astype(F32),
+        pick_row,
+        preferred_element_type=F32,
+        precision=lax.Precision.HIGHEST,
+    )
+    target = jnp.sum(jnp.where(step_row[0:4], spread, 0.0), axis=0, keepdims=True)
+    target = target - ((n * 16 + mp) * 512).astype(F32)
+    target_v[...] = jnp.broadcast_to(target, (8, 256))
+
     row_i, col_i = iota((128, 128), 0), iota((128, 128), 1)
     limit = jnp.zeros((128, 128), jnp.int32)
     for r in range(4):
@@ -346,7 +359,7 @@
     lax.fori_loop(0, 7, send_one, 0)
 
     def two(half, k):
-        ref = full.at[c, pl.ds(half * 4, 4), v, u]
+        ref = full.at[c, pl.ds(half * 2, 2), v, u]
         return rcopy(
             ref, ref, two_send.at[half], two_recv.at[half], at_uv((u + k) % 4, v)
         )
@@ -361,7 +374,7 @@
         ref = full.at[cc, zz]
         return rcopy(ref, ref, relay_send.at[zz], relay_recv.at[zz], sibling)
 
-    for half in range(2):
+    for half in range(4):
 
         def wait_one(zz, carry):
             @pl.when(zz != 3)
@@ -370,14 +383,14 @@
 
             return carry
 
-        lax.fori_loop(half * 4, half * 4 + 4, wait_one, 0)
+        lax.fori_loop(half * 2, half * 2 + 2, wait_one, 0)
         for k in range(1, 4):
             two(half, k).start()
 
     am_advance(2)
 
     def two_all(half):
-        ref = full.at[c, pl.ds(half * 4, 4), v, pl.ds(0, 3)]
+        ref = full.at[c, pl.ds(half * 2, 2), v, pl.ds(0, 3)]
         return rcopy(ref, ref, two_send.at[half], two_recv.at[half], sibling)
 
     def send_three(zz, carry):
@@ -385,8 +398,9 @@
             three(k, zz, v).start()
         return carry
 
-    two_all(0).wait_recv()
-    lax.fori_loop(0, 4, send_three, 0)
+    for half in range(2):
+        two_all(half).wait_recv()
+        lax.fori_loop(half * 2, half * 2 + 2, send_three, 0)
     am_advance(3)
 
     loads[3].wait()
@@ -417,6 +431,9 @@
     lax.fori_loop(0, 7, am_block, 0)
     ones = jnp.ones((8, 128), F32)
 
+    def chosen_here():
+        return iota((512, 256), 0).astype(F32) == target_v[0:1, :]
+
     def inverse_norm(ref, width):
         sums = lax.dot_general(
             ones, ref[...], NT, preferred_element_type=F32, precision=lax.Precision.HIGHEST
@@ -503,7 +520,8 @@
         p_all(which).wait_send()
         z_all(which).wait_send()
 
-    two_all(1).wait_recv()
+    two_all(2).wait_recv()
+    two_all(3).wait_recv()
     loads[4].wait()
 
     def gather_block(zz, carry):
@@ -556,7 +574,8 @@
     acc_a[...] = logits_a
     top_a = jnp.max(logits_a, axis=0, keepdims=True)
     total_a = jnp.sum(jnp.exp(logits_a - top_a), axis=0, keepdims=True)
-    start_pair(1, (top_a, total_a))
+    picked_a = jnp.sum(jnp.where(chosen_here(), logits_a, 0.0), axis=0, keepdims=True)
+    start_pair(1, (top_a, total_a, picked_a))
     lax.fori_loop(4, 6, gather_block, 0)
     start_p(1)
     lax.fori_loop(6, 9, gather_block, 0)
@@ -564,24 +583,14 @@
     logits_e = acc_e[...] * inverse_norm(square_e, 8192.0)
     top_e = jnp.max(logits_e, axis=0, keepdims=True)
     total_e = jnp.sum(jnp.exp(logits_e - top_e), axis=0, keepdims=True)
-    difference = logits_e - CONTRAST * acc_a[...]
-    pick_row = (iota((64, 256), 1) // 4 == iota((64, 256), 0)).astype(F32)
-    step_row = iota((8, 256), 1) % 4 == iota((8, 256), 0)
-    spread = jnp.dot(
-        chosen[...].astype(F32),
-        pick_row,
-        preferred_element_type=F32,
-        precision=lax.Precision.HIGHEST,
-    )
-    target = jnp.sum(jnp.where(step_row[0:4], spread, 0.0), axis=0, keepdims=True)
-    target = target - ((n * 16 + mp) * 512).astype(F32)
-    matched = iota((512, 256), 0).astype(F32) == target
-    picked = jnp.sum(jnp.where(matched, difference, 0.0), axis=0, keepdims=True)
+    picked = jnp.sum(jnp.where(chosen_here(), logits_e, 0.0), axis=0, keepdims=True)
 
     start_pair(0, (top_e, total_e, picked))
     start_p(0)
     start_z(1)
-    diff[...] = difference.T
+    diff[...] = (logits_e - CONTRAST * acc_a[...]).T
+    store = pltpu.make_async_copy(diff, out_diff, load_sem.at[10])
+    store.start()
 
     state_all.wait_send()
     attended_all.wait_send()
@@ -592,7 +601,7 @@
     part_all.wait_send()
     ref = full.at[c, pl.ds(0, 7), v, u]
     rcopy(ref, ref, one_send, one_recv.at[0], sibling).wait_send()
-    for half in range(2):
+    for half in range(4):
         two_all(half).wait_send()
 
     def drain(k, carry):
@@ -606,26 +615,29 @@
     start_z(0)
     settle(1)
     z_all(1).wait_recv()
-    top, total, _ = join([stats_z[1, k] for k in range(8)])
+    top, total, pick_a = join([stats_z[1, k] for k in range(8)])
     lse_a = top + jnp.log(total)
     z_all(0).wait_recv()
     top, total, pick = join([stats_z[0, k] for k in range(8)])
     shift = top + jnp.log(total) - CONTRAST * lse_a
-    chosen_row = pick - shift
+    chosen_row = pick - CONTRAST * pick_a - shift
     shift = jnp.concatenate([shift[0:1], shift[1:2]], axis=1)
     chosen_row = jnp.concatenate([chosen_row[0:1], chosen_row[1:2]], axis=1)
-    shift_t = jnp.broadcast_to(shift, (128, 256)).T
-    out[...] = (diff[...] - shift_t[:, 0:1]).reshape(64, 4, 512).astype(BF16)
-    masked = jnp.where(step_row, chosen_row, 0.0)
+    row_8 = iota((8, 256), 0)
+    out_rows[...] = jnp.where(row_8 == 0, shift, jnp.where(row_8 == 1, chosen_row, 0.0))
+    store.wait()
+    settle(0)
+
+
+def finish(diff, rows, out, out_chosen):
+    shift = jnp.broadcast_to(rows[0:1, :], (128, 256)).T
+    out[...] = (diff[...] - shift[:, 0:1]).reshape(64, 4, 512).astype(BF16)
+    pick_row = (iota((64, 256), 1) // 4 == iota((64, 256), 0)).astype(F32)
+    step_row = iota((8, 256), 1) % 4 == iota((8, 256), 0)
+    masked = jnp.where(step_row, rows[1:2, :], 0.0)
     out_chosen[...] = lax.dot_general(
         masked, pick_row, NT, preferred_element_type=F32, precision=lax.Precision.HIGHEST
     )[0:4]
-    settle(0)
-
-
-def finish(scores, chosen_score, out, out_chosen):
-    out[...] = scores[...]
-    out_chosen[...] = chosen_score[...]
 
 
 def local(
@@ -647,11 +659,11 @@
     vmem = pl.BlockSpec(memory_space=pltpu.VMEM)
     hbm = pl.BlockSpec(memory_space=pl.ANY)
     dma = pltpu.SemaphoreType.DMA
-    scores, chosen_score = pl.pallas_call(
+    diff, rows = pl.pallas_call(
         kernel,
         out_shape=(
-            jax.ShapeDtypeStruct((64, 4, 512), BF16),
-            jax.ShapeDtypeStruct((4, 64), F32),
+            jax.ShapeDtypeStruct((256, 512), F32),
+            jax.ShapeDtypeStruct((8, 256), F32),
         ),
         in_specs=[pl.BlockSpec(memory_space=pltpu.SMEM)]
         + [hbm] * 4
@@ -659,7 +671,7 @@
         + [hbm]
         + [vmem]
         + [hbm] * 5,
-        out_specs=(vmem, vmem),
+        out_specs=(hbm, vmem),
         scratch_shapes=[
             pltpu.VMEM((4, 4, 8192), BF16),
             pltpu.VMEM((4, 4, 1024), BF16),
@@ -683,17 +695,18 @@
             pltpu.VMEM((256, 128), F32),
             pltpu.VMEM((256, 128), F32),
             pltpu.VMEM((256, 512), F32),
+            pltpu.VMEM((8, 256), F32),
             pltpu.VMEM((2, 2, 8, 128), F32),
             pltpu.VMEM((2, 16, 8, 128), F32),
             pltpu.VMEM((2, 8, 8, 128), F32),
-            dma((10,)),
+            dma((11,)),
             dma((2,)),
             dma((2,)),
             dma((2,)),
             dma,
             dma((8,)),
-            dma((2,)),
-            dma((2,)),
+            dma((4,)),
+            dma((4,)),
             dma((8,)),
             dma((4, 8)),
             dma((8,)),
@@ -734,7 +747,7 @@
         in_specs=[vmem] * 2,
         out_specs=(vmem, vmem),
         name="finish",
-    )(scores, chosen_score)
+    )(diff, rows)
     return scores, chosen_score.T
 
 

time: 75.5 us -> 74.5 us (0.987)
  Pallas kernels: 74.3 us -> 73.4 us
    pallas_call x1, Pallas kernels: 72.6 us -> 71.4 us  [local(): pl.pallas_call(kernel, out_shape=(jax.ShapeDtypeStruct((256, 512), F32),...]
where the time goes in v5:
time: 74.5 us; the launch traced here: 74 us
  Pallas kernels  73.4 us (99%)
    pallas_call x1, Pallas kernels, local(): pl.pallas_call(kernel, out_shape=(jax.ShapeDtypeStruct((256, 512), F32),...  71.4 us
    pallas_call x1, Pallas kernels, local(): pl.pallas_call(finish, out_shape=(jax.ShapeDtypeStruct((64, 4, 512), BF16...  1.98 us

profile of v5, /device:TPU:1, one launch (start us, length us, event | category | flops | bytes accessed | tf_op | source)
XLA Modules:
  0.0 74.0 jit_solution(15241005588591792149)
XLA Ops:
  0.6 71.4 %contrast.1 = (f32[256,512]{1,0:T(8,128)}, f32[8,256]{1,0:T(8,128)}) custom-call(s32[8]{0:T(128)} %lengths.1, bf16[8,4,8192]{2,1,0:T(4,128)(2,1)} %queries.1, bf16[8,4,1024]{2,1,0:T(4,128)(2,1)} %new_keys.1, bf16[8,4,1024]{2,1,0:T(4,128)(2,1)} %new_values.1, bf16[256,512]{1,0:T(8,128)(2,1)} %resid.1, bf16[512]{0:T(512)(128)(2,1)} %gain_expert.1, ...), custom_call_target="tpu_custom_call" | custom-call | tf_op jit(solution)/shard_map/contrast/pallas_call | solution.py:662
  72.1 2.0 %finish.1 = (bf16[64,4,512]{2,1,0:T(4,128)(2,1)}, f32[4,64]{1,0:T(4,128)}) custom-call(f32[256,512]{1,0:T(8,128)} %get-tuple-element.6.diff, f32[8,256]{1,0:T(8,128)} %get-tuple-element.7.rows), custom_call_target="tpu_custom_call" | custom-call | tf_op jit(solution)/shard_map/finish/pallas_call | solution.py:741

commit v6 on v5

--- a/solution.py
+++ b/solution.py
@@ -353,7 +353,8 @@
         )
 
     def send_one(k, carry):
-        one((11 - hop(k)) % 8, (z + hop(k)) % 8).start()
+        slot = k + (k + 1) // 4 - k // 7
+        one(slot, (z + 11 - slot) % 8).start()
         return carry
 
     lax.fori_loop(0, 7, send_one, 0)

time: 74.5 us -> 74.1 us (level)
  no operation moved by 1% of the time
where the time goes in v6:
time: 74.1 us; the launch traced here: 73.8 us
  Pallas kernels  73.2 us (99%)
    pallas_call x1, Pallas kernels, local(): pl.pallas_call(kernel, out_shape=(jax.ShapeDtypeStruct((256, 512), F32),...  71.2 us
    pallas_call x1, Pallas kernels, local(): pl.pallas_call(finish, out_shape=(jax.ShapeDtypeStruct((64, 4, 512), BF16...  1.98 us

profile of v6, /device:TPU:1, one launch (start us, length us, event | category | flops | bytes accessed | tf_op | source)
XLA Modules:
  0.0 73.8 jit_solution(13650145395069240129)
XLA Ops:
  0.6 71.2 %contrast.1 = (f32[256,512]{1,0:T(8,128)}, f32[8,256]{1,0:T(8,128)}) custom-call(s32[8]{0:T(128)} %lengths.1, bf16[8,4,8192]{2,1,0:T(4,128)(2,1)} %queries.1, bf16[8,4,1024]{2,1,0:T(4,128)(2,1)} %new_keys.1, bf16[8,4,1024]{2,1,0:T(4,128)(2,1)} %new_values.1, bf16[256,512]{1,0:T(8,128)(2,1)} %resid.1, bf16[512]{0:T(512)(128)(2,1)} %gain_expert.1, ...), custom_call_target="tpu_custom_call" | custom-call | tf_op jit(solution)/shard_map/contrast/pallas_call | solution.py:663
  71.8 2.0 %finish.1 = (bf16[64,4,512]{2,1,0:T(4,128)(2,1)}, f32[4,64]{1,0:T(4,128)}) custom-call(f32[256,512]{1,0:T(8,128)} %get-tuple-element.6.diff, f32[8,256]{1,0:T(8,128)} %get-tuple-element.7.rows), custom_call_target="tpu_custom_call" | custom-call | tf_op jit(solution)/shard_map/finish/pallas_call | solution.py:742
